TPU v7x, 32 devices: a whole 2x2x4 slice. The times are simulated.
32 devices in a mesh: grp: 4 (over z), tile: 8 (over y, x, core).
Axes of the slice: x: 2, y: 2, z: 4, core: 2. Of those that a mesh axis runs over, the one named last changes fastest.
Arguments:
- embeddings: bfloat16 [12288, 1024], P(('grp', 'tile'))
- row_group: int32 [12288], P(('grp', 'tile')), may hold values from 0 to 3, as said below
- row_cluster: int32 [12288], P(('grp', 'tile')), may hold values from 0 to 1
Outputs:
- best_match: float32 [12288], P(('grp', 'tile'))
Inputs may be any that keep to these rules, and one draw needn't show every extreme that they name: `row_group`: among the rows of one device no group is named by more than 192 rows; for every index along tile some group is named by exactly 192 rows on every device of that tile index.
All inputs are finite; a program needn't handle non-finite values.
Results may differ from a plain program's by a relative error of at most 0.00053.
Values may be sent and summed in bfloat16 or wider, within the bound.
A program may use at most 128 MiB of HBM per device.

v0:
```python
import jax
import jax.numpy as jnp
from jax import lax
from jax.sharding import PartitionSpec as P

epsilon = 1e-06


def unit_rows(values):
    floats = values.astype(jnp.float32)
    scaled = floats * lax.rsqrt(jnp.sum(floats * floats, axis=-1, keepdims=True) + epsilon)
    return scaled.astype(jnp.bfloat16)


def slot_index(owners, groups, capacity):
    onehot = (owners[:, None] == jnp.arange(groups, dtype=jnp.int32)[None, :]).astype(jnp.int32)
    earlier = jnp.cumsum(onehot, axis=0) - onehot
    ranked = jnp.sum(earlier * onehot, axis=1)
    return owners * capacity + ranked


def masked_table(scores, left_ids, right_ids, left_pos, right_pos):
    allowed = (
        (left_ids[:, None] == right_ids[None, :])
        & (right_ids[None, :] >= 0)
        & (left_pos[:, None] != right_pos[None, :])
    )
    return jnp.where(allowed, scores, jnp.float32(-1.0))


def local(embeddings, row_group, row_cluster):
    row_count = embeddings.shape[0]
    columns = embeddings.shape[1]
    groups = lax.axis_size("grp")
    capacity = 2 * row_count // groups
    slots_all = groups * capacity
    placed = slot_index(row_group, groups, capacity)
    normed = unit_rows(embeddings)
    outgoing = (
        jnp.zeros((slots_all, columns), jnp.bfloat16)
        .at[placed]
        .set(normed)
        .reshape(groups, capacity, columns)
    )
    out_tags = (
        jnp.full((slots_all,), -1, jnp.int32).at[placed].set(row_cluster).reshape(groups, capacity)
    )
    members, member_ids = (
        lax.all_to_all(outgoing, "grp", split_axis=0, concat_axis=0, tiled=True),
        lax.all_to_all(out_tags, "grp", split_axis=0, concat_axis=0, tiled=True),
    )
    members = members.reshape(slots_all, columns)
    member_ids = member_ids.reshape(slots_all)
    tile_here = lax.axis_index("tile")
    local_pos = jnp.arange(slots_all, dtype=jnp.int32)
    own_pos = tile_here * slots_all + local_pos
    start_best = jnp.full((slots_all,), -1.0, jnp.float32)
    piece_rows = lax.all_gather(members, "tile", axis=0, tiled=True)
    piece_ids = lax.all_gather(member_ids, "tile", axis=0, tiled=True)
    scores = jnp.einsum("id,jd->ij", members, piece_rows, preferred_element_type=jnp.float32)
    piece_pos = jnp.arange(piece_rows.shape[0], dtype=jnp.int32)
    best_sim = jnp.maximum(
        start_best, jnp.max(masked_table(scores, member_ids, piece_ids, own_pos, piece_pos), axis=1)
    )
    results = best_sim.reshape(groups, capacity)
    arrived = lax.all_to_all(results, "grp", split_axis=0, concat_axis=0, tiled=True)
    return jnp.take(arrived.reshape(slots_all), placed)


def solution(mesh):
    placed = (P(("grp", "tile"), None), P(("grp", "tile")), P(("grp", "tile")))
    return jax.shard_map(
        local, mesh=mesh, in_specs=placed, out_specs=P(("grp", "tile")), check_vma=False
    )
```

profile of v0, /device:TPU:0, one launch (start us, length us, event | category | flops | bytes accessed | tf_op | source)
XLA Modules:
  0.0 165.6 jit_solution(2397317870342657456)
XLA Ops:
  6.5 0.0 all-gather.3.cloned.1.call-start
  6.5 0.7 fusion.7
  7.2 1.2 reduce-window.6
  8.4 0.2 slice_reduce_fusion
  8.6 0.2 reduce-window.9
  8.8 0.1 add_bitcast_fusion
  8.9 0.7 fusion.10
  9.6 0.7 compare_select_fusion
  10.3 1.4 fusion.1
  11.7 3.2 %scatter_custom_fusion.1 = bf16[768,1024]{1,0:T(8,128)(2,1)S(1)} fusion(s32[384]{0:T(512)S(1)} %compare_select_fusion, bf16[384,1024]{1,0:T(8,128)(2,1)} %param.3, f32[384]{0:T(512)S(1)} %add_rsqrt_fusion, bf16[]{:T(256)} %constant.18.clone.1), kind=kCustom, calls=%fused_computation.10 | custom fusion | flops 1179648 | bytes 2361346 | tf_op jit(solution)/shard_map/scatter | solution.py:42
  14.9 43.2 %all_to_all.20 = bf16[4,192,1024]{2,1,0:T(8,128)(2,1)} all-to-all(bf16[4,192,1024]{2,1,0:T(8,128)(2,1)S(1)} %bitcast.27), channel_id=1, replica_groups=mesh['grp'=4,'tile'=8] {'grp'}, dimensions={0} | all-to-all | bytes 3145728 | tf_op jit(solution)/shard_map/all_to_all | solution.py:49
  58.1 0.0 all-gather.3.cloned.1.call-update
  58.1 3.1 %scatter_custom_fusion = s32[768]{0:T(1024)S(1)} fusion(s32[384]{0:T(512)S(1)} %compare_select_fusion, s32[384]{0:T(512)} %param.5, s32[]{:T(128)} %constant.10.clone.1), kind=kCustom, calls=%fused_computation.28 | custom fusion | bytes 3584 | tf_op jit(solution)/shard_map/scatter | solution.py:46
  61.2 0.7 all_to_all.13
  61.9 3.2 %all-to-all-start = ((s32[4,1,192]{2,1,0:T(1,128)}), s32[4,1,192]{2,1,0:T(1,128)S(1)}, u32[]{:S(2)}, u32[]{:S(2)}) async-start(s32[4,1,192]{2,1,0:T(1,128)} %all_to_all.13), calls=%async_computation | async-start | bytes 8192 | tf_op jit(solution)/shard_map/all_to_all | solution.py:50
  65.1 5.5 %all-to-all-done = s32[4,1,192]{2,1,0:T(1,128)S(1)} async-done(((s32[4,1,192]{2,1,0:T(1,128)}), s32[4,1,192]{2,1,0:T(1,128)S(1)}, u32[]{:S(2)}, u32[]{:S(2)}) %all-to-all-start) | async-done | bytes 3104 | tf_op jit(solution)/shard_map/all_to_all | solution.py:50
  70.7 0.1 reshape.99
  70.8 0.1 eq.45
  70.8 9.1 %all-gather = s32[8,1,768]{2,1,0:T(1,128)S(1)} all-gather(s32[1,1,768]{2,1,0:T(1,128)S(1)} %reshape.99), channel_id=1, replica_groups=mesh['grp'=4,'tile'=8] {'tile'}, dimensions={0}, use_global_device_ids=true | all-gather | bytes 27648 | tf_op jit(solution)/shard_map/all_gather | solution.py:59
  80.0 49.6 %all-gather.3.cloned.1.call-done = bf16[6144,1024]{1,0:T(8,128)(2,1)} async-done(((bf16[768,1024]{1,0:T(8,128)(2,1)}), bf16[6144,1024]{1,0:T(8,128)(2,1)}) %all-gather.3.cloned.1.call-update) | async-done | bytes 12582928 | tf_op jit(solution)/shard_map/all_gather | solution.py:58
  129.6 15.8 %select_reduce_fusion = f32[768]{0:T(1024)S(1)} fusion(bf16[768,1024]{1,0:T(8,128)(2,1)} %bitcast.26, bf16[6144,1024]{1,0:T(8,128)(2,1)} %all-gather.3.cloned.1.call-done, s32[768]{0:T(1024)S(1)} %iota_add_fusion, s32[6144]{0:T(1024)S(1)} %bitcast.29, s32[768]{0:T(1024)S(1)} %eq.45, pred[6144]{0:T(1024)(128)(4,1)S(1)} %broadcast_compare_fusion), kind=kOutput, calls=%fused_computation.3 | convolution fusion | flops 9691986944 | bytes 14195712 | tf_op jit(solution)/shard_map/id,jd->ij/dot_general | solution.py:60
  145.4 0.7 max_broadcast_in_dim.15
  146.1 4.6 %all-to-all-start.2 = ((f32[4,1,192]{2,1,0:T(1,128)}), f32[4,1,192]{2,1,0:T(1,128)S(1)}, u32[]{:S(2)}, u32[]{:S(2)}) async-start(f32[4,1,192]{2,1,0:T(1,128)} %max_broadcast_in_dim.15), calls=%async_computation.2 | async-start | bytes 8192 | tf_op jit(solution)/shard_map/all_to_all | solution.py:66
  150.7 5.6 %all-to-all-done.2 = f32[4,1,192]{2,1,0:T(1,128)S(1)} async-done(((f32[4,1,192]{2,1,0:T(1,128)}), f32[4,1,192]{2,1,0:T(1,128)S(1)}, u32[]{:S(2)}, u32[]{:S(2)}) %all-to-all-start.2) | async-done | bytes 3104 | tf_op jit(solution)/shard_map/all_to_all | solution.py:66
  156.2 0.1 reshape.71
  156.3 1.9 %gather_fusion = f32[384]{0:T(512)S(1)} fusion(f32[768]{0:T(1024)S(1)} %reshape.71, s32[1024]{0:T(1024)S(1)} %pad_clamp_fusion), kind=kCustom, calls=%fused_computation | custom fusion | bytes 4608 | tf_op jit(solution)/shard_map/jit(_take)/gather | solution.py:67
  158.2 0.6 and_select_fusion
  (7 shorter events, 0.1 us)
Async XLA Ops:
  6.5 123.1 %all-gather.3.cloned.1.call-start = ((), (), s32[]{:S(2)}) async-start(), calls=%async_computation.3 | async-start | bytes 14155776 | tf_op jit(solution)/shard_map/all_gather | solution.py:58
  61.9 8.8 %all-to-all-start = ((s32[4,1,192]{2,1,0:T(1,128)}), s32[4,1,192]{2,1,0:T(1,128)S(1)}, u32[]{:S(2)}, u32[]{:S(2)}) async-start(s32[4,1,192]{2,1,0:T(1,128)} %all_to_all.13), calls=%async_computation | async-start | bytes 8192 | tf_op jit(solution)/shard_map/all_to_all | solution.py:50
  146.1 10.2 %all-to-all-start.2 = ((f32[4,1,192]{2,1,0:T(1,128)}), f32[4,1,192]{2,1,0:T(1,128)S(1)}, u32[]{:S(2)}, u32[]{:S(2)}) async-start(f32[4,1,192]{2,1,0:T(1,128)} %max_broadcast_in_dim.15), calls=%async_computation.2 | async-start | bytes 8192 | tf_op jit(solution)/shard_map/all_to_all | solution.py:66
Sparse Core Ops, SparseCore 0:
  58.2 71.3 all-gather.2
where the time goes:
time: 166 us
  waiting for transfers between devices  60.7 us (37%)
  blocking collectives  52.3 us (32%)
  matrix products  15.8 us (10%)
  between operations  13.5 us (8%)
  other arithmetic  8.78 us (5%)
  starting transfers between devices  7.83 us (5%)
  local copies, waits for them, and re-layouts  6.77 us (4%)
    all_gather x1, waiting for transfers between devices, local(): piece_rows = lax.all_gather(members, 'tile', axis=0, tiled=True)  49.6 us
    all_to_all x1, blocking collectives, local(): lax.all_to_all(outgoing, 'grp', split_axis=0, concat_axis=0, tiled=True)  43.2 us
    dot_general x1, matrix products, local(): jnp.einsum('id,jd->ij', members, piece_rows, preferred_element_type=jnp.f...  15.8 us
    all_gather x1, blocking collectives, local(): piece_ids = lax.all_gather(member_ids, 'tile', axis=0, tiled=True)  9.1 us
    all_to_all x1, waiting for transfers between devices, local(): lax.all_to_all(results, 'grp', split_axis=0, concat_axis=0, tiled=True)  5.57 us
    all_to_all x1, waiting for transfers between devices, local(): lax.all_to_all(out_tags, 'grp', split_axis=0, concat_axis=0, tiled=True)  5.53 us
    all_to_all x1, starting transfers between devices, local(): lax.all_to_all(results, 'grp', split_axis=0, concat_axis=0, tiled=True)  4.59 us
  transfers between devices with their start and end apart: 3, of which 3 were waited for; matrix products, arithmetic and copies ran while one was open for 2% of the time, Pallas kernels for 0%

commit v1 on v0

--- a/solution.py
+++ b/solution.py
@@ -1,9 +1,15 @@
+import functools
+
 import jax
 import jax.numpy as jnp
 from jax import lax
+from jax.experimental import pallas as pl
+from jax.experimental.pallas import tpu as pltpu
 from jax.sharding import PartitionSpec as P
 
+MESH = pl.DeviceIdType.MESH
 epsilon = 1e-06
+NT = (((1,), (1,)), ((), ()))
 
 
 def unit_rows(values):
@@ -28,7 +34,7 @@
     return jnp.where(allowed, scores, jnp.float32(-1.0))
 
 
-def local(embeddings, row_group, row_cluster):
+def local_general(embeddings, row_group, row_cluster):
     row_count = embeddings.shape[0]
     columns = embeddings.shape[1]
     groups = lax.axis_size("grp")
@@ -67,8 +73,256 @@
     return jnp.take(arrived.reshape(slots_all), placed)
 
 
+def kernel(
+    x_ref, owner_ref, cluster_ref, out_ref,
+    normed, send, queries, keys, tag_out, tag_in, tag_own, tag_far, best, result_in,
+    ztag_s, ztag_r, z_s, z_r, ftag_s, ftag_r, sib_s, sib_r, near_s, near_r, relay_s, relay_r, res_s, res_r,
+):
+    rows = x_ref.shape[0]
+    groups = 4
+    cap = 2 * rows // groups
+    slots = groups * cap
+    half = cap // 2
+    me = lax.axis_index("grp")
+    tile = lax.axis_index("tile")
+    core = lax.rem(tile, 2)
+    xpos = lax.rem(tile // 2, 2)
+    ypos = tile // 4
+    sib = tile + 1 - 2 * core
+    xstep = 2 - 4 * xpos
+    ystep = 4 - 8 * ypos
+    near = (tile + xstep, tile + ystep)
+    far = tile + xstep + ystep
+
+    def other(r):
+        return lax.rem(me + r, groups)
+
+    partners = [(other(r), tile) for r in (1, 2, 3)]
+    partners += [(other(r), sib) for r in (0, 1, 2, 3)]
+    partners += [(me, near[0]), (me, near[1]), (me, far)]
+    barrier = pltpu.get_barrier_semaphore()
+    for partner in partners:
+        pl.semaphore_signal(barrier, inc=1, device_id=partner, device_id_type=MESH)
+
+    def remote(src, dst, ssem, rsem, device):
+        return pltpu.make_async_remote_copy(
+            src_ref=src, dst_ref=dst, send_sem=ssem, recv_sem=rsem, device_id=device, device_id_type=MESH
+        )
+
+    owner = owner_ref[...]
+    cluster = cluster_ref[...]
+    group_of = lax.broadcasted_iota(jnp.int32, (8, rows), 0)
+    belongs = group_of == owner
+    before = lax.broadcasted_iota(jnp.int32, (rows, rows), 0) < lax.broadcasted_iota(jnp.int32, (rows, rows), 1)
+    earlier = jnp.dot(
+        jnp.where(belongs, 1.0, 0.0).astype(jnp.bfloat16),
+        jnp.where(before, 1.0, 0.0).astype(jnp.bfloat16),
+        preferred_element_type=jnp.float32,
+    )
+    rank = jnp.sum(jnp.where(belongs, earlier, 0.0), axis=0, keepdims=True).astype(jnp.int32)
+    slot = owner * cap + rank
+    place = me * cap + rank
+    at_place = jnp.where(lax.broadcasted_iota(jnp.int32, (slots, rows), 0) == place, 1.0, 0.0).astype(jnp.bfloat16)
+
+    marks = jnp.where(belongs, (cluster + 1).astype(jnp.float32), 0.0).astype(jnp.bfloat16)
+    tag_out[...] = lax.dot_general(marks, at_place, NT, preferred_element_type=jnp.float32)
+
+    chunk = rows // 4
+    for c in range(4):
+        part = pl.ds(c * chunk, chunk)
+        normed[part, :] = unit_rows(x_ref[part, :])
+
+    pl.semaphore_wait(barrier, len(partners))
+
+    ztags = []
+    for r in (1, 2, 3):
+        copy = remote(tag_out, tag_in.at[r - 1], ztag_s.at[r - 1], ztag_r.at[r - 1], (other(groups - r), tile))
+        copy.start()
+        ztags.append(copy)
+
+    def filled(group):
+        sel = lax.broadcasted_iota(jnp.int32, (cap, rows), 0) + group * cap
+        sel = jnp.where(sel == slot, 1.0, 0.0).astype(jnp.bfloat16)
+        return jnp.dot(sel, normed[...], preferred_element_type=jnp.float32).astype(jnp.bfloat16)
+
+    def piece(r):
+        return pl.ds(pl.multiple_of(other(r) * cap, cap), cap)
+
+    zcopies = {}
+    for r in (2, 3, 1):
+        send[r - 1] = filled(other(groups - r))
+        copy = remote(
+            send.at[r - 1], queries.at[piece(0), :], z_s.at[r - 1], z_r.at[r - 1], (other(groups - r), tile)
+        )
+        copy.start()
+        zcopies[r] = copy
+    queries[piece(0), :] = filled(me)
+
+    pending = []
+
+    def arrival(r):
+        return remote(send.at[r - 1], queries.at[piece(r), :], z_s.at[r - 1], z_r.at[r - 1], (other(groups - r), tile))
+
+    def spread(i, r):
+        src = queries.at[piece(r), :]
+        copies = [
+            remote(src, queries.at[pl.ds(pl.multiple_of(slots + other(r) * cap, cap), cap), :],
+                   sib_s.at[i], sib_r.at[i], (me, sib)),
+            remote(src, keys.at[0, piece(r), :], near_s.at[0, i], near_r.at[0, i], (me, near[0])),
+            remote(src, keys.at[1, piece(r), :], near_s.at[1, i], near_r.at[1, i], (me, near[1])),
+        ]
+        for copy in copies[::-1]:
+            copy.start()
+        return copies
+
+    def relay(i, r, copies):
+        made = []
+        for n in (0, 1):
+            copies[1 + n].wait_recv()
+            lines = pl.ds(pl.multiple_of(other(r) * cap + n * half, half), half)
+            copy = remote(keys.at[n, lines, :], keys.at[2, lines, :], relay_s.at[n, i], relay_r.at[n, i], (me, near[1 - n]))
+            copy.start()
+            made.append(copy)
+        return made
+
+    order = (0, 1, 3, 2)
+    spreads, relays = [spread(0, 0)], []
+
+    for copy in ztags:
+        copy.wait_recv()
+    total = tag_out[...] + tag_in[0] + tag_in[1] + tag_in[2]
+    mine = jnp.sum(jnp.where(lax.broadcasted_iota(jnp.int32, (8, slots), 0) == me, total, 0.0), axis=0, keepdims=True)
+    tag_own[...] = jnp.broadcast_to(mine, (8, slots))
+    ftags = []
+    for n, device in enumerate((sib, near[0], near[1], far)):
+        copy = remote(tag_own, tag_far.at[n], ftag_s.at[n], ftag_r.at[n], (me, device))
+        copy.start()
+        ftags.append(copy)
+
+    for i in (1, 2, 3):
+        zcopies[order[i]].wait_recv()
+        spreads.append(spread(i, order[i]))
+        relays.append(relay(i - 1, order[i - 1], spreads[i - 1]))
+
+    for copy in ftags:
+        copy.wait_recv()
+    for copies in spreads:
+        copies[0].wait_recv()
+
+    best[...] = jnp.full(best.shape, -1.0, jnp.float32)
+
+    def compare(keys_at, key_tags, own_first):
+        lines = keys_at[...]
+        for h in (0, 1):
+            scores = lax.dot_general(
+                lines, queries[h * slots : (h + 1) * slots, :], NT, preferred_element_type=jnp.float32
+            )
+            query_tags = tag_own[0:1, :] if h == 0 else tag_far[0, 0:1, :]
+            allowed = key_tags == query_tags
+            if h == 0 and own_first is not None:
+                row_at = lax.broadcasted_iota(jnp.int32, (cap, slots), 0) + own_first
+                allowed = allowed & (row_at != lax.broadcasted_iota(jnp.int32, (cap, slots), 1))
+            found = jnp.max(jnp.where(allowed, scores, -1.0), axis=0, keepdims=True)
+            best[h] = jnp.maximum(best[h], found)
+
+    def column(tags, r):
+        lanes = lax.broadcasted_iota(jnp.int32, (cap, slots), 1)
+        wanted = lax.broadcasted_iota(jnp.int32, (cap, slots), 0) + other(r) * cap
+        picked = jnp.sum(jnp.where(lanes == wanted, tags, 0.0), axis=1, keepdims=True)
+        return jnp.where(picked > 0.0, picked, -1.0)
+
+    def step(i):
+        return lax.select(i < 2, i, 5 - i)
+
+    @pl.loop(0, 4)
+    def _(i):
+        r = step(i)
+        compare(queries.at[piece(r), :], column(tag_own[0:1, :], r), other(r) * cap)
+
+    relays.append(relay(3, order[3], spreads[3]))
+
+    for n in (0, 1):
+        @pl.loop(0, 4)
+        def _(i):
+            r = step(i)
+            compare(keys.at[n, piece(r), :], column(tag_far[1 + n, 0:1, :], r), None)
+
+    for i in range(4):
+        for copy in relays[i]:
+            copy.wait_recv()
+        r = order[i]
+        compare(keys.at[2, piece(r), :], column(tag_far[3, 0:1, :], r), None)
+
+    copies = []
+    for h, device in enumerate((tile, sib)):
+        for r in range(4):
+            index = h * 4 + r
+            if index == 0:
+                result_in[0] = best[0]
+                continue
+            copy = remote(best.at[h], result_in.at[index], res_s.at[index], res_r.at[index], (other(groups - r), device))
+            copy.start()
+            copies.append(copy)
+    for copy in copies:
+        copy.wait_recv()
+
+    out = jnp.zeros((1, rows), jnp.float32)
+    for r in range(4):
+        block = jnp.maximum(result_in[r], result_in[4 + r])
+        high = block.astype(jnp.bfloat16)
+        rest = block - high.astype(jnp.float32)
+        middle = rest.astype(jnp.bfloat16)
+        low = (rest - middle.astype(jnp.float32)).astype(jnp.bfloat16)
+        picked = [
+            jnp.dot(term, at_place, preferred_element_type=jnp.float32)[0:1, :] for term in (high, middle, low)
+        ]
+        value = (picked[0] + picked[1]) + picked[2]
+        out = jnp.where(owner == other(r), value, out)
+    out_ref[...] = out
+
+    for copy in ztags + ftags + copies + list(zcopies.values()):
+        copy.wait_send()
+    for group in spreads + relays:
+        for copy in group:
+            copy.wait_send()
+
+
+def local_fused(embeddings, row_group, row_cluster):
+    rows, columns = embeddings.shape
+    slots = 2 * rows
+    dma = pltpu.SemaphoreType.DMA
+    out = pl.pallas_call(
+        kernel,
+        out_shape=jax.ShapeDtypeStruct((1, rows), jnp.float32),
+        in_specs=[pl.BlockSpec(memory_space=pltpu.VMEM)] * 3,
+        out_specs=pl.BlockSpec(memory_space=pltpu.VMEM),
+        scratch_shapes=[
+            pltpu.VMEM((rows, columns), jnp.bfloat16),
+            pltpu.VMEM((3, slots // 4, columns), jnp.bfloat16),
+            pltpu.VMEM((2 * slots, columns), jnp.bfloat16),
+            pltpu.VMEM((3, slots, columns), jnp.bfloat16),
+            pltpu.VMEM((8, slots), jnp.float32),
+            pltpu.VMEM((3, 8, slots), jnp.float32),
+            pltpu.VMEM((8, slots), jnp.float32),
+            pltpu.VMEM((4, 8, slots), jnp.float32),
+            pltpu.VMEM((2, 8, slots), jnp.float32),
+            pltpu.VMEM((8, 8, slots), jnp.float32),
+            dma((3,)), dma((3,)), dma((3,)), dma((3,)),
+            dma((4,)), dma((4,)), dma((4,)), dma((4,)),
+            dma((2, 4)), dma((2, 4)), dma((2, 4)), dma((2, 4)),
+            dma((8,)), dma((8,)),
+        ],
+        compiler_params=pltpu.CompilerParams(
+            collective_id=0, has_side_effects=True, vmem_limit_bytes=48 * 1024 * 1024
+        ),
+    )(embeddings, row_group.reshape(1, rows), row_cluster.reshape(1, rows))
+    return out.reshape(rows)
+
+
 def solution(mesh):
+    fused = mesh.shape["grp"] == 4 and mesh.shape["tile"] == 8
     placed = (P(("grp", "tile"), None), P(("grp", "tile")), P(("grp", "tile")))
     return jax.shard_map(
-        local, mesh=mesh, in_specs=placed, out_specs=P(("grp", "tile")), check_vma=False
-    )
+        local_fused if fused else local_general,
+        mesh=mesh, in_specs=placed, out_specs=P(("grp", "tile")), check_vma=False,
+    )

time: 166 us -> 101 us (0.61)
  Pallas kernels: 0 us -> 98 us
  waiting for transfers between devices: 60.7 us -> 0 us
  blocking collectives: 52.3 us -> 0 us
  matrix products: 15.8 us -> 0 us
  between operations: 13.5 us -> 0.01 us
  other arithmetic: 8.78 us -> 0.6 us
  starting transfers between devices: 7.83 us -> 0 us
  local copies, waits for them, and re-layouts: 6.77 us -> 1.83 us
    pallas_call x0 -> x1, Pallas kernels: none -> 98 us  [local_fused(): pl.pallas_call(kernel, out_shape=jax.ShapeDtypeStruct((1, rows), jnp.floa...]
    all_gather x1 -> x0, waiting for transfers between devices: 49.6 us -> none  [local(): piece_rows = lax.all_gather(members, 'tile', axis=0, tiled=True)]
    all_to_all x1 -> x0, blocking collectives: 43.2 us -> none  [local(): lax.all_to_all(outgoing, 'grp', split_axis=0, concat_axis=0, tiled=True)]
    dot_general x1 -> x0, matrix products: 15.8 us -> none  [local(): jnp.einsum('id,jd->ij', members, piece_rows, preferred_element_type=jnp.f...]
    all_to_all x2 -> x0, waiting for transfers between devices: 11.1 us -> none  [the longest x1 5.57 us: local(): lax.all_to_all(results, 'grp', split_axis=0, concat_axis=0, tiled=True)]
    all_gather x1 -> x0, blocking collectives: 9.1 us -> none  [local(): piece_ids = lax.all_gather(member_ids, 'tile', axis=0, tiled=True)]
    all_to_all x2 -> x0, starting transfers between devices: 7.82 us -> none  [the longest x1 4.59 us: local(): lax.all_to_all(results, 'grp', split_axis=0, concat_axis=0, tiled=True)]
    scatter x1 -> x0, other arithmetic: 3.22 us -> none  [local(): outgoing = jnp.zeros((slots_all, columns), jnp.bfloat16).at[placed].set(n...]
  transfers between devices with their start and end apart: 3 -> 0, of which waited for: 3 -> 0; matrix products, arithmetic and copies ran while one was open for 2% -> 0% of each run, Pallas kernels for 0% -> 0%
where the time goes in v1:
time: 101 us; the launch traced here: 100 us
  Pallas kernels  98 us (97%)
  local copies, waits for them, and re-layouts  1.83 us (2%)
    pallas_call x1, Pallas kernels, local_fused(): pl.pallas_call(kernel, out_shape=jax.ShapeDtypeStruct((1, rows), jnp.floa...  98 us

profile of v1, /device:TPU:0, one launch (start us, length us, event | category | flops | bytes accessed | tf_op | source)
XLA Modules:
  0.0 100.5 jit_solution(6197535234431375459)
XLA Ops:
  0.0 0.0 copy-start.1
  0.0 0.7 reshape.9.owner_ref
  0.7 0.0 copy-done.1
  0.7 0.0 copy-start
  0.7 1.1 %copy-done = bf16[384,1024]{1,0:T(8,128)(2,1)S(1)} copy-done((bf16[384,1024]{1,0:T(8,128)(2,1)S(1)}, bf16[384,1024]{1,0:T(8,128)(2,1)}, u32[]{:S(2)}) %copy-start) | copy-done | bytes 786456
  1.8 98.0 %shard_map.37 = f32[1,384]{1,0:T(1,128)S(1)} custom-call(bf16[384,1024]{1,0:T(8,128)(2,1)S(1)} %copy-done, s32[1,384]{1,0:T(1,128)S(1)} %reshape.9.owner_ref, s32[1,384]{1,0:T(1,128)S(1)} %reshape.10.cluster_ref), custom_call_target="tpu_custom_call" | custom-call | tf_op jit(solution)/shard_map/pallas_call | solution.py:294
  99.9 0.6 reduce
  (1 shorter events, 0.0 us)
Async XLA Ops:
  0.0 0.7 copy-start.1
  0.7 1.1 %copy-start = (bf16[384,1024]{1,0:T(8,128)(2,1)S(1)}, bf16[384,1024]{1,0:T(8,128)(2,1)}, u32[]{:S(2)}) copy-start(bf16[384,1024]{1,0:T(8,128)(2,1)} %x_ref.1) | copy-start | bytes 2359300

commit v2 on v1

--- a/solution.py
+++ b/solution.py
@@ -1,5 +1,3 @@
-import functools
-
 import jax
 import jax.numpy as jnp
 from jax import lax
@@ -75,7 +73,7 @@
 
 def kernel(
     x_ref, owner_ref, cluster_ref, out_ref,
-    normed, send, queries, keys, tag_out, tag_in, tag_own, tag_far, best, result_in,
+    normed, send, queries, keys, tag_out, tag_in, tag_own, tag_far, query_tags, key_tags, best, result_out, result_in,
     ztag_s, ztag_r, z_s, z_r, ftag_s, ftag_r, sib_s, sib_r, near_s, near_r, relay_s, relay_r, res_s, res_r,
 ):
     rows = x_ref.shape[0]
@@ -83,6 +81,7 @@
     cap = 2 * rows // groups
     slots = groups * cap
     half = cap // 2
+    width = query_tags.shape[2]
     me = lax.axis_index("grp")
     tile = lax.axis_index("tile")
     core = lax.rem(tile, 2)
@@ -93,12 +92,10 @@
     ystep = 4 - 8 * ypos
     near = (tile + xstep, tile + ystep)
     far = tile + xstep + ystep
-
-    def other(r):
-        return lax.rem(me + r, groups)
-
-    partners = [(other(r), tile) for r in (1, 2, 3)]
-    partners += [(other(r), sib) for r in (0, 1, 2, 3)]
+    peer = (me, me + 1 - 2 * lax.rem(me, 2), me + 2 - 4 * (me // 2), 3 - me)
+
+    partners = [(peer[r], tile) for r in (1, 2, 3)]
+    partners += [(peer[r], sib) for r in (0, 1, 2, 3)]
     partners += [(me, near[0]), (me, near[1]), (me, far)]
     barrier = pltpu.get_barrier_semaphore()
     for partner in partners:
@@ -136,7 +133,7 @@
 
     ztags = []
     for r in (1, 2, 3):
-        copy = remote(tag_out, tag_in.at[r - 1], ztag_s.at[r - 1], ztag_r.at[r - 1], (other(groups - r), tile))
+        copy = remote(tag_out, tag_in.at[r - 1], ztag_s.at[r - 1], ztag_r.at[r - 1], (peer[r], tile))
         copy.start()
         ztags.append(copy)
 
@@ -146,47 +143,42 @@
         return jnp.dot(sel, normed[...], preferred_element_type=jnp.float32).astype(jnp.bfloat16)
 
     def piece(r):
-        return pl.ds(pl.multiple_of(other(r) * cap, cap), cap)
-
-    zcopies = {}
-    for r in (2, 3, 1):
-        send[r - 1] = filled(other(groups - r))
-        copy = remote(
-            send.at[r - 1], queries.at[piece(0), :], z_s.at[r - 1], z_r.at[r - 1], (other(groups - r), tile)
-        )
-        copy.start()
-        zcopies[r] = copy
-    queries[piece(0), :] = filled(me)
-
-    pending = []
-
-    def arrival(r):
-        return remote(send.at[r - 1], queries.at[piece(r), :], z_s.at[r - 1], z_r.at[r - 1], (other(groups - r), tile))
-
-    def spread(i, r):
-        src = queries.at[piece(r), :]
+        return pl.ds(pl.multiple_of(peer[r] * cap, cap), cap)
+
+    def zcopy(r):
+        return remote(send.at[r - 1], queries.at[piece(0), :], z_s.at[r - 1], z_r.at[r - 1], (peer[r], tile))
+
+    def spread(i):
+        src = queries.at[piece(i), :]
+        beside = pl.ds(pl.multiple_of(slots + peer[i] * cap, cap), cap)
+        line = pl.ds(i * cap, cap)
         copies = [
-            remote(src, queries.at[pl.ds(pl.multiple_of(slots + other(r) * cap, cap), cap), :],
-                   sib_s.at[i], sib_r.at[i], (me, sib)),
-            remote(src, keys.at[0, piece(r), :], near_s.at[0, i], near_r.at[0, i], (me, near[0])),
-            remote(src, keys.at[1, piece(r), :], near_s.at[1, i], near_r.at[1, i], (me, near[1])),
+            remote(src, queries.at[beside, :], sib_s.at[i], sib_r.at[i], (me, sib)),
+            remote(src, keys.at[0, line, :], near_s.at[0, i], near_r.at[0, i], (me, near[0])),
+            remote(src, keys.at[1, line, :], near_s.at[1, i], near_r.at[1, i], (me, near[1])),
         ]
         for copy in copies[::-1]:
             copy.start()
         return copies
 
-    def relay(i, r, copies):
+    def relay(i, copies):
         made = []
         for n in (0, 1):
             copies[1 + n].wait_recv()
-            lines = pl.ds(pl.multiple_of(other(r) * cap + n * half, half), half)
-            copy = remote(keys.at[n, lines, :], keys.at[2, lines, :], relay_s.at[n, i], relay_r.at[n, i], (me, near[1 - n]))
+            line = pl.ds(i * cap + n * half, half)
+            copy = remote(keys.at[n, line, :], keys.at[2, line, :], relay_s.at[n, i], relay_r.at[n, i], (me, near[1 - n]))
             copy.start()
             made.append(copy)
         return made
 
-    order = (0, 1, 3, 2)
-    spreads, relays = [spread(0, 0)], []
+    zcopies = {}
+    for r in (2, 1):
+        send[r - 1] = filled(peer[r])
+        zcopies[r] = zcopy(r)
+        zcopies[r].start()
+    queries[piece(0), :] = filled(me)
+    spreads, relays = [spread(0)], []
+    send[2] = filled(peer[3])
 
     for copy in ztags:
         copy.wait_recv()
@@ -199,68 +191,84 @@
         copy.start()
         ftags.append(copy)
 
-    for i in (1, 2, 3):
-        zcopies[order[i]].wait_recv()
-        spreads.append(spread(i, order[i]))
-        relays.append(relay(i - 1, order[i - 1], spreads[i - 1]))
+    relays.append(relay(0, spreads[0]))
+    zcopies[2].wait_send()
+    zcopies[3] = zcopy(3)
+    zcopies[3].start()
+    zcopies[1].wait_recv()
+    spreads.append(spread(1))
+    zcopies[2].wait_recv()
+    spreads.append(spread(2))
+
+    def column(tags, sources, n):
+        for i in range(groups):
+            lanes = lax.broadcasted_iota(jnp.int32, (cap, slots), 1)
+            wanted = lax.broadcasted_iota(jnp.int32, (cap, slots), 0) + sources[i] * cap
+            picked = jnp.sum(jnp.where(lanes == wanted, tags, 0.0), axis=1, keepdims=True)
+            picked = jnp.where(picked > 0.0, picked, -1.0)
+            key_tags[n, i * cap : (i + 1) * cap, :] = jnp.broadcast_to(picked, (cap, 128))
 
     for copy in ftags:
         copy.wait_recv()
+    for c in range(slots // width):
+        query_tags[c] = tag_own[:, c * width : (c + 1) * width]
+        query_tags[slots // width + c] = tag_far[0, :, c * width : (c + 1) * width]
+    column(tag_own[0:1, :], range(groups), 3)
+    for n in (0, 1, 2):
+        column(tag_far[1 + n, 0:1, :], peer, n)
+    best[...] = jnp.full(best.shape, -1.0, jnp.float32)
+
+    relays.append(relay(1, spreads[1]))
+    relays.append(relay(2, spreads[2]))
+    zcopies[3].wait_recv()
+    spreads.append(spread(3))
     for copies in spreads:
         copies[0].wait_recv()
 
-    best[...] = jnp.full(best.shape, -1.0, jnp.float32)
-
-    def compare(keys_at, key_tags, own_first):
-        lines = keys_at[...]
-        for h in (0, 1):
-            scores = lax.dot_general(
-                lines, queries[h * slots : (h + 1) * slots, :], NT, preferred_element_type=jnp.float32
-            )
-            query_tags = tag_own[0:1, :] if h == 0 else tag_far[0, 0:1, :]
-            allowed = key_tags == query_tags
-            if h == 0 and own_first is not None:
-                row_at = lax.broadcasted_iota(jnp.int32, (cap, slots), 0) + own_first
-                allowed = allowed & (row_at != lax.broadcasted_iota(jnp.int32, (cap, slots), 1))
+    def compare(source, n, first, count, own):
+        @pl.loop(0, 2 * slots // width)
+        def _(c):
+            asked = queries[pl.ds(pl.multiple_of(c * width, width), width), :]
+            scores = lax.dot_general(source[...], asked, NT, preferred_element_type=jnp.float32)
+            tags = key_tags[n, first : first + count, :]
+            allowed = jnp.concatenate([tags] * (width // 128), axis=1) == query_tags[c, 0:1, :]
+            if own:
+                line = lax.broadcasted_iota(jnp.int32, (count, width), 0)
+                lane = lax.broadcasted_iota(jnp.int32, (count, width), 1) + c * width
+                allowed = allowed & (line != lane)
             found = jnp.max(jnp.where(allowed, scores, -1.0), axis=0, keepdims=True)
-            best[h] = jnp.maximum(best[h], found)
-
-    def column(tags, r):
-        lanes = lax.broadcasted_iota(jnp.int32, (cap, slots), 1)
-        wanted = lax.broadcasted_iota(jnp.int32, (cap, slots), 0) + other(r) * cap
-        picked = jnp.sum(jnp.where(lanes == wanted, tags, 0.0), axis=1, keepdims=True)
-        return jnp.where(picked > 0.0, picked, -1.0)
-
-    def step(i):
-        return lax.select(i < 2, i, 5 - i)
-
-    @pl.loop(0, 4)
-    def _(i):
-        r = step(i)
-        compare(queries.at[piece(r), :], column(tag_own[0:1, :], r), other(r) * cap)
-
-    relays.append(relay(3, order[3], spreads[3]))
-
-    for n in (0, 1):
-        @pl.loop(0, 4)
-        def _(i):
-            r = step(i)
-            compare(keys.at[n, piece(r), :], column(tag_far[1 + n, 0:1, :], r), None)
-
-    for i in range(4):
-        for copy in relays[i]:
+            best[c] = jnp.maximum(best[c], found)
+
+    def key_part(n, first, last):
+        compare(keys.at[n, first * cap : last * cap, :], n, first * cap, (last - first) * cap, False)
+
+    compare(queries.at[0:slots, :], 3, 0, slots, True)
+    key_part(0, 0, 3)
+    key_part(1, 0, 3)
+    relays.append(relay(3, spreads[3]))
+    for made in relays[:3]:
+        for copy in made:
             copy.wait_recv()
-        r = order[i]
-        compare(keys.at[2, piece(r), :], column(tag_far[3, 0:1, :], r), None)
-
+    key_part(2, 0, 3)
+    key_part(0, 3, 4)
+    key_part(1, 3, 4)
+    for copy in relays[3]:
+        copy.wait_recv()
+    key_part(2, 3, 4)
+
+    for h in (0, 1):
+        for c in range(slots // width):
+            result_out[h, :, c * width : (c + 1) * width] = best[h * (slots // width) + c]
     copies = []
     for h, device in enumerate((tile, sib)):
         for r in range(4):
             index = h * 4 + r
             if index == 0:
-                result_in[0] = best[0]
+                result_in[0] = result_out[0]
                 continue
-            copy = remote(best.at[h], result_in.at[index], res_s.at[index], res_r.at[index], (other(groups - r), device))
+            copy = remote(
+                result_out.at[h], result_in.at[index], res_s.at[index], res_r.at[index], (peer[r], device)
+            )
             copy.start()
             copies.append(copy)
     for copy in copies:
@@ -277,10 +285,10 @@
             jnp.dot(term, at_place, preferred_element_type=jnp.float32)[0:1, :] for term in (high, middle, low)
         ]
         value = (picked[0] + picked[1]) + picked[2]
-        out = jnp.where(owner == other(r), value, out)
+        out = jnp.where(owner == peer[r], value, out)
     out_ref[...] = out
 
-    for copy in ztags + ftags + copies + list(zcopies.values()):
+    for copy in ztags + ftags + copies + [zcopies[1], zcopies[3]]:
         copy.wait_send()
     for group in spreads + relays:
         for copy in group:
@@ -290,6 +298,7 @@
 def local_fused(embeddings, row_group, row_cluster):
     rows, columns = embeddings.shape
     slots = 2 * rows
+    width = 256
     dma = pltpu.SemaphoreType.DMA
     out = pl.pallas_call(
         kernel,
@@ -305,6 +314,9 @@
             pltpu.VMEM((3, 8, slots), jnp.float32),
             pltpu.VMEM((8, slots), jnp.float32),
             pltpu.VMEM((4, 8, slots), jnp.float32),
+            pltpu.VMEM((2 * slots // width, 8, width), jnp.float32),
+            pltpu.VMEM((4, slots, 128), jnp.float32),
+            pltpu.VMEM((2 * slots // width, 8, width), jnp.float32),
             pltpu.VMEM((2, 8, slots), jnp.float32),
             pltpu.VMEM((8, 8, slots), jnp.float32),
             dma((3,)), dma((3,)), dma((3,)), dma((3,)),

time: 101 us -> 78.4 us (0.78)
  Pallas kernels: 98 us -> 75.8 us
    pallas_call x1, Pallas kernels: 98 us -> 75.8 us  [local_fused(): pl.pallas_call(kernel, out_shape=jax.ShapeDtypeStruct((1, rows), jnp.floa...]
where the time goes in v2:
time: 78.4 us; the launch traced here: 78.2 us
  Pallas kernels  75.8 us (97%)
  local copies, waits for them, and re-layouts  1.83 us (2%)
    pallas_call x1, Pallas kernels, local_fused(): pl.pallas_call(kernel, out_shape=jax.ShapeDtypeStruct((1, rows), jnp.floa...  75.8 us

profile of v2, /device:TPU:0, one launch (start us, length us, event | category | flops | bytes accessed | tf_op | source)
XLA Modules:
  0.0 78.2 jit_solution(17337136864741587951)
XLA Ops:
  0.0 0.0 copy-start.1
  0.0 0.7 reshape.9.owner_ref
  0.7 0.0 copy-done.1
  0.7 0.0 copy-start
  0.7 1.1 %copy-done = bf16[384,1024]{1,0:T(8,128)(2,1)S(1)} copy-done((bf16[384,1024]{1,0:T(8,128)(2,1)S(1)}, bf16[384,1024]{1,0:T(8,128)(2,1)}, u32[]{:S(2)}) %copy-start) | copy-done | bytes 786456
  1.8 75.8 %shard_map.37 = f32[1,384]{1,0:T(1,128)S(1)} custom-call(bf16[384,1024]{1,0:T(8,128)(2,1)S(1)} %copy-done, s32[1,384]{1,0:T(1,128)S(1)} %reshape.9.owner_ref, s32[1,384]{1,0:T(1,128)S(1)} %reshape.10.cluster_ref), custom_call_target="tpu_custom_call" | custom-call | tf_op jit(solution)/shard_map/pallas_call | solution.py:303
  77.6 0.6 reduce
  (1 shorter events, 0.0 us)
Async XLA Ops:
  0.0 0.7 copy-start.1
  0.7 1.1 %copy-start = (bf16[384,1024]{1,0:T(8,128)(2,1)S(1)}, bf16[384,1024]{1,0:T(8,128)(2,1)}, u32[]{:S(2)}) copy-start(bf16[384,1024]{1,0:T(8,128)(2,1)} %x_ref.1) | copy-start | bytes 2359300

commit v3 on v2

v3 whole, which is shorter than its diff:
```python
import jax
import jax.numpy as jnp
from jax import lax
from jax.experimental import pallas as pl
from jax.experimental.pallas import tpu as pltpu
from jax.sharding import PartitionSpec as P

MESH = pl.DeviceIdType.MESH
epsilon = 1e-06
NT = (((1,), (1,)), ((), ()))


def unit_rows(values):
    floats = values.astype(jnp.float32)
    scaled = floats * lax.rsqrt(jnp.sum(floats * floats, axis=-1, keepdims=True) + epsilon)
    return scaled.astype(jnp.bfloat16)


def slot_index(owners, groups, capacity):
    onehot = (owners[:, None] == jnp.arange(groups, dtype=jnp.int32)[None, :]).astype(jnp.int32)
    earlier = jnp.cumsum(onehot, axis=0) - onehot
    ranked = jnp.sum(earlier * onehot, axis=1)
    return owners * capacity + ranked


def masked_table(scores, left_ids, right_ids, left_pos, right_pos):
    allowed = (
        (left_ids[:, None] == right_ids[None, :])
        & (right_ids[None, :] >= 0)
        & (left_pos[:, None] != right_pos[None, :])
    )
    return jnp.where(allowed, scores, jnp.float32(-1.0))


def local_general(embeddings, row_group, row_cluster):
    row_count = embeddings.shape[0]
    columns = embeddings.shape[1]
    groups = lax.axis_size("grp")
    capacity = 2 * row_count // groups
    slots_all = groups * capacity
    placed = slot_index(row_group, groups, capacity)
    normed = unit_rows(embeddings)
    outgoing = (
        jnp.zeros((slots_all, columns), jnp.bfloat16)
        .at[placed]
        .set(normed)
        .reshape(groups, capacity, columns)
    )
    out_tags = (
        jnp.full((slots_all,), -1, jnp.int32).at[placed].set(row_cluster).reshape(groups, capacity)
    )
    members, member_ids = (
        lax.all_to_all(outgoing, "grp", split_axis=0, concat_axis=0, tiled=True),
        lax.all_to_all(out_tags, "grp", split_axis=0, concat_axis=0, tiled=True),
    )
    members = members.reshape(slots_all, columns)
    member_ids = member_ids.reshape(slots_all)
    tile_here = lax.axis_index("tile")
    local_pos = jnp.arange(slots_all, dtype=jnp.int32)
    own_pos = tile_here * slots_all + local_pos
    start_best = jnp.full((slots_all,), -1.0, jnp.float32)
    piece_rows = lax.all_gather(members, "tile", axis=0, tiled=True)
    piece_ids = lax.all_gather(member_ids, "tile", axis=0, tiled=True)
    scores = jnp.einsum("id,jd->ij", members, piece_rows, preferred_element_type=jnp.float32)
    piece_pos = jnp.arange(piece_rows.shape[0], dtype=jnp.int32)
    best_sim = jnp.maximum(
        start_best, jnp.max(masked_table(scores, member_ids, piece_ids, own_pos, piece_pos), axis=1)
    )
    results = best_sim.reshape(groups, capacity)
    arrived = lax.all_to_all(results, "grp", split_axis=0, concat_axis=0, tiled=True)
    return jnp.take(arrived.reshape(slots_all), placed)


def kernel(
    x_ref, owner_ref, cluster_ref, out_ref,
    normed, send, members, tag_out, tag_in, tags, query_tags, key_tags, best, result_out, result_in, picks,
    ztag_s, ztag_r, z_s, z_r, ptag_s, ptag_r, sib_s, sib_r, near_s, near_r, relay_s, relay_r, res_s, res_r,
):
    rows = x_ref.shape[0]
    groups = 4
    cap = 2 * rows // groups
    slots = groups * cap
    half = slots // 2
    me = lax.axis_index("grp")
    tile = lax.axis_index("tile")
    core = lax.rem(tile, 2)
    xpos = lax.rem(tile // 2, 2)
    ypos = tile // 4
    beside = 1 - 2 * core
    sib = tile + beside
    xdev = tile + 2 - 4 * xpos
    ydev = tile + 4 - 8 * ypos
    cross = 4 - xpos
    crossdev = ydev + (1 - xpos) * beside
    peer = (me, me + 1 - 2 * lax.rem(me, 2), me + 2 - 4 * (me // 2), 3 - me)
    early = me // 2
    late = 1 - early

    partners = [(peer[r], tile) for r in (1, 2, 3)]
    partners += [(peer[r], device) for r in range(4) for device in (sib, xdev, ydev, ydev + beside)]
    barrier = pltpu.get_barrier_semaphore()
    for partner in partners:
        pl.semaphore_signal(barrier, inc=1, device_id=partner, device_id_type=MESH)

    def remote(src, dst, ssem, rsem, device):
        return pltpu.make_async_remote_copy(
            src_ref=src, dst_ref=dst, send_sem=ssem, recv_sem=rsem, device_id=device, device_id_type=MESH
        )

    owner = owner_ref[...]
    cluster = cluster_ref[...]
    group_of = lax.broadcasted_iota(jnp.int32, (8, rows), 0)
    belongs = group_of == owner
    before = lax.broadcasted_iota(jnp.int32, (rows, rows), 0) < lax.broadcasted_iota(jnp.int32, (rows, rows), 1)
    earlier = jnp.dot(
        jnp.where(belongs, 1.0, 0.0).astype(jnp.bfloat16),
        jnp.where(before, 1.0, 0.0).astype(jnp.bfloat16),
        preferred_element_type=jnp.float32,
    )
    rank = jnp.sum(jnp.where(belongs, earlier, 0.0), axis=0, keepdims=True).astype(jnp.int32)
    slot = owner * cap + rank
    place = me * cap + rank
    at_place = jnp.where(lax.broadcasted_iota(jnp.int32, (slots, rows), 0) == place, 1.0, 0.0).astype(jnp.bfloat16)

    marks = jnp.where(belongs, (cluster + 1).astype(jnp.float32), 0.0).astype(jnp.bfloat16)
    tag_out[...] = lax.dot_general(marks, at_place, NT, preferred_element_type=jnp.float32)

    chunk = rows // 4
    for c in range(4):
        part = pl.ds(c * chunk, chunk)
        normed[part, :] = unit_rows(x_ref[part, :])

    pl.semaphore_wait(barrier, len(partners))

    ztags = []
    for r in (1, 2, 3):
        copy = remote(tag_out, tag_in.at[r - 1], ztag_s.at[r - 1], ztag_r.at[r - 1], (peer[r], tile))
        copy.start()
        ztags.append(copy)

    def filled(group):
        sel = lax.broadcasted_iota(jnp.int32, (cap, rows), 0) + group * cap
        sel = jnp.where(sel == slot, 1.0, 0.0).astype(jnp.bfloat16)
        return jnp.dot(sel, normed[...], preferred_element_type=jnp.float32).astype(jnp.bfloat16)

    def piece(r):
        return pl.ds(pl.multiple_of(peer[r] * cap, cap), cap)

    def zcopy(r):
        return remote(send.at[r - 1], members.at[0, piece(0), :], z_s.at[r - 1], z_r.at[r - 1], (peer[r], tile))

    def spread(r):
        src = members.at[0, piece(r), :]
        copies = [
            remote(src, members.at[1, piece(r), :], sib_s.at[r], sib_r.at[r], (me, sib)),
            remote(src, members.at[2, piece(r), :], near_s.at[0, r], near_r.at[0, r], (me, xdev)),
            remote(src, members.at[3, piece(r), :], near_s.at[1, r], near_r.at[1, r], (me, ydev)),
        ]
        for copy in copies[::-1]:
            copy.start()
        return copies

    def relay(r, copies):
        copies[2].wait_recv()
        copy = remote(members.at[3, piece(r), :], members.at[4, piece(r), :], relay_s.at[r], relay_r.at[r], (me, sib))
        copy.start()
        return copy

    zcopies = {}
    for r in (2, 1):
        send[r - 1] = filled(peer[r])
        zcopies[r] = zcopy(r)
        zcopies[r].start()
    members[0, piece(0), :] = filled(me)
    spreads, relays = [spread(0)], []
    send[2] = filled(peer[3])

    for copy in ztags:
        copy.wait_recv()
    total = tag_out[...] + tag_in[0] + tag_in[1] + tag_in[2]
    tags[0] = jnp.sum(
        jnp.where(lax.broadcasted_iota(jnp.int32, (8, slots), 0) == me, total, 0.0), axis=0, keepdims=True
    )
    ptags = []
    for n, device in enumerate((sib, xdev, ydev, ydev + beside)):
        copy = remote(tags.at[0], tags.at[1 + n], ptag_s.at[n], ptag_r.at[n], (me, device))
        copy.start()
        ptags.append(copy)

    zcopies[2].wait_send()
    zcopies[3] = zcopy(3)
    zcopies[3].start()
    zcopies[1].wait_recv()
    spreads.append(spread(1))
    zcopies[2].wait_recv()
    spreads.append(spread(2))
    relays.append(relay(0, spreads[0]))

    for copy in ptags:
        copy.wait_recv()
    best[...] = jnp.full(best.shape, -1.0, jnp.float32)
    for n in range(5):
        row = tags[n]
        query_tags[n, 0] = row[:, :half]
        query_tags[n, 1] = row[:, half:]
        for i in range(groups):
            first = i * cap // 128 * 128
            lanes = lax.broadcasted_iota(jnp.int32, (cap, 256), 1) + (first - i * cap)
            wanted = lax.broadcasted_iota(jnp.int32, (cap, 256), 0)
            picked = jnp.sum(jnp.where(lanes == wanted, row[:, first : first + 256], 0.0), axis=1, keepdims=True)
            picked = jnp.where(picked > 0.0, picked, -1.0)
            key_tags[n, i * cap : (i + 1) * cap, :] = jnp.broadcast_to(picked, (cap, 128))

    def compare(kblock, khalf, qblock, qhalf, to, own=False):
        lines = pl.ds(pl.multiple_of(khalf * half, half), half)
        asked = members[qblock, pl.ds(pl.multiple_of(qhalf * half, half), half), :]
        scores = lax.dot_general(members[kblock, lines, :], asked, NT, preferred_element_type=jnp.float32)
        key_tag = jnp.concatenate([key_tags[kblock, lines, :]] * (half // 128), axis=1)
        allowed = key_tag == query_tags[qblock, qhalf]
        if own:
            line = lax.broadcasted_iota(jnp.int32, (half, half), 0) + (khalf * half + (kblock + qblock) * 2 * slots)
            lane = lax.broadcasted_iota(jnp.int32, (half, half), 1) + qhalf * half
            allowed = allowed & (line != lane)
        found = jnp.max(jnp.where(allowed, scores, -1.0), axis=0, keepdims=True)
        best[to, qhalf] = jnp.maximum(best[to, qhalf], found)

    relays.append(relay(1, spreads[1]))
    for copies in spreads[:2]:
        copies[0].wait_recv()
        copies[1].wait_recv()

    @pl.loop(0, 6)
    def _(i):
        j = i // 2
        q = lax.rem(i, 2)
        compare(j + (j + 1) // 2, early, q, early, q, own=True)

    for copy in relays[:2]:
        copy.wait_recv()

    @pl.loop(0, 2)
    def _(q):
        compare(cross + q * (2 - cross), early, 2 + q * (cross - 2), early, 2 + q)

    relays.append(relay(2, spreads[2]))
    zcopies[3].wait_recv()
    spreads.append(spread(3))
    for copies in spreads[2:]:
        copies[0].wait_recv()

    @pl.loop(0, 6)
    def _(i):
        j = i // 2
        q = lax.rem(i, 2)
        compare(j + (j + 1) // 2, early, q, late, q, own=True)

    @pl.loop(0, 4)
    def _(i):
        q = lax.rem(i, 2)
        compare(0, late, q, i // 2, q, own=True)

    relays.append(relay(3, spreads[3]))
    for copies in spreads[2:]:
        copies[1].wait_recv()

    @pl.loop(0, 8)
    def _(i):
        q = lax.rem(i, 2)
        compare(2 + i // 4, late, q, lax.rem(i // 2, 2), q)

    for copy in relays[2:]:
        copy.wait_recv()

    @pl.loop(0, 6)
    def _(i):
        q = lax.rem(i, 2)
        m = i // 2
        compare(
            cross + q * (2 - cross), early + (late - early) * (1 - lax.rem(m, 2)),
            2 + q * (cross - 2), early + (late - early) * ((m + 1) // 2), 2 + q,
        )

    copies = []
    for h, device in enumerate((tile, sib, xdev, crossdev)):
        result_out[h] = jnp.concatenate([best[h, 0], best[h, 1]], axis=1)
        for r in (3, 2, 1, 0):
            index = h * 4 + r
            if index == 0:
                result_in[0] = result_out[0]
                continue
            copy = remote(
                result_out.at[h], result_in.at[index], res_s.at[index], res_r.at[index], (peer[r], device)
            )
            copy.start()
            copies.append(copy)
    for copy in copies:
        copy.wait_recv()

    picks[...] = jnp.zeros(picks.shape, jnp.float32)
    for r in range(4):
        block = jnp.maximum(
            jnp.maximum(result_in[r], result_in[4 + r]), jnp.maximum(result_in[8 + r], result_in[12 + r])
        )
        high = block.astype(jnp.bfloat16).astype(jnp.float32)
        middle = (block - high).astype(jnp.bfloat16).astype(jnp.float32)
        picks[r : r + 1, :] = high
        picks[4 + r : 5 + r, :] = middle
        picks[8 + r : 9 + r, :] = (block - high) - middle
    found = jnp.dot(picks[...].astype(jnp.bfloat16), at_place, preferred_element_type=jnp.float32)
    out = jnp.zeros((1, rows), jnp.float32)
    for r in range(4):
        value = (found[r : r + 1, :] + found[4 + r : 5 + r, :]) + found[8 + r : 9 + r, :]
        out = jnp.where(owner == peer[r], value, out)
    out_ref[...] = out

    for copy in ztags + ptags + copies + relays + [zcopies[1], zcopies[3]]:
        copy.wait_send()
    for group in spreads:
        for copy in group:
            copy.wait_send()


def local_fused(embeddings, row_group, row_cluster):
    rows, columns = embeddings.shape
    slots = 2 * rows
    dma = pltpu.SemaphoreType.DMA
    out = pl.pallas_call(
        kernel,
        out_shape=jax.ShapeDtypeStruct((1, rows), jnp.float32),
        in_specs=[pl.BlockSpec(memory_space=pltpu.VMEM)] * 3,
        out_specs=pl.BlockSpec(memory_space=pltpu.VMEM),
        scratch_shapes=[
            pltpu.VMEM((rows, columns), jnp.bfloat16),
            pltpu.VMEM((3, slots // 4, columns), jnp.bfloat16),
            pltpu.VMEM((5, slots, columns), jnp.bfloat16),
            pltpu.VMEM((8, slots), jnp.float32),
            pltpu.VMEM((3, 8, slots), jnp.float32),
            pltpu.VMEM((5, 1, slots), jnp.float32),
            pltpu.VMEM((5, 2, 1, slots // 2), jnp.float32),
            pltpu.VMEM((5, slots, 128), jnp.float32),
            pltpu.VMEM((4, 2, 1, slots // 2), jnp.float32),
            pltpu.VMEM((4, 1, slots), jnp.float32),
            pltpu.VMEM((16, 1, slots), jnp.float32),
            pltpu.VMEM((16, slots), jnp.float32),
            dma((3,)), dma((3,)), dma((3,)), dma((3,)),
            dma((4,)), dma((4,)), dma((4,)), dma((4,)),
            dma((2, 4)), dma((2, 4)), dma((4,)), dma((4,)),
            dma((16,)), dma((16,)),
        ],
        compiler_params=pltpu.CompilerParams(
            collective_id=0, has_side_effects=True, vmem_limit_bytes=48 * 1024 * 1024
        ),
    )(embeddings, row_group.reshape(1, rows), row_cluster.reshape(1, rows))
    return out.reshape(rows)


def solution(mesh):
    fused = mesh.shape["grp"] == 4 and mesh.shape["tile"] == 8
    placed = (P(("grp", "tile"), None), P(("grp", "tile")), P(("grp", "tile")))
    return jax.shard_map(
        local_fused if fused else local_general,
        mesh=mesh, in_specs=placed, out_specs=P(("grp", "tile")), check_vma=False,
    )
```

time: 78.4 us -> 69.9 us (0.89)
  Pallas kernels: 75.8 us -> 67.2 us
    pallas_call x1, Pallas kernels: 75.8 us -> 67.2 us  [local_fused(): pl.pallas_call(kernel, out_shape=jax.ShapeDtypeStruct((1, rows), jnp.floa...]
where the time goes in v3:
time: 69.9 us; the launch traced here: 69.7 us
  Pallas kernels  67.2 us (96%)
  local copies, waits for them, and re-layouts  1.83 us (3%)
    pallas_call x1, Pallas kernels, local_fused(): pl.pallas_call(kernel, out_shape=jax.ShapeDtypeStruct((1, rows), jnp.floa...  67.2 us

profile of v3, /device:TPU:0, one launch (start us, length us, event | category | flops | bytes accessed | tf_op | source)
XLA Modules:
  0.0 69.7 jit_solution(3697617831833102371)
XLA Ops:
  0.0 0.0 copy-start.1
  0.0 0.7 reshape.9.owner_ref
  0.7 0.0 copy-done.1
  0.7 0.0 copy-start
  0.7 1.1 %copy-done = bf16[384,1024]{1,0:T(8,128)(2,1)S(1)} copy-done((bf16[384,1024]{1,0:T(8,128)(2,1)S(1)}, bf16[384,1024]{1,0:T(8,128)(2,1)}, u32[]{:S(2)}) %copy-start) | copy-done | bytes 786456
  1.8 67.2 %shard_map.37 = f32[1,384]{1,0:T(1,128)S(1)} custom-call(bf16[384,1024]{1,0:T(8,128)(2,1)S(1)} %copy-done, s32[1,384]{1,0:T(1,128)S(1)} %reshape.9.owner_ref, s32[1,384]{1,0:T(1,128)S(1)} %reshape.10.cluster_ref), custom_call_target="tpu_custom_call" | custom-call | tf_op jit(solution)/shard_map/pallas_call | solution.py:327
  69.1 0.6 reduce
  (1 shorter events, 0.0 us)
Async XLA Ops:
  0.0 0.7 %copy-start.1 = (s32[384]{0:T(512)S(1)}, s32[384]{0:T(512)}, u32[]{:S(2)}) copy-start(s32[384]{0:T(512)} %param.5) | copy-start | bytes 4612
  0.7 1.1 %copy-start = (bf16[384,1024]{1,0:T(8,128)(2,1)S(1)}, bf16[384,1024]{1,0:T(8,128)(2,1)}, u32[]{:S(2)}) copy-start(bf16[384,1024]{1,0:T(8,128)(2,1)} %x_ref.1) | copy-start | bytes 2359300

commit v4 on v3

v4 whole, which is shorter than its diff:
```python
import jax
import jax.numpy as jnp
from jax import lax
from jax.experimental import pallas as pl
from jax.experimental.pallas import tpu as pltpu
from jax.sharding import PartitionSpec as P

MESH = pl.DeviceIdType.MESH
epsilon = 1e-06
NT = (((1,), (1,)), ((), ()))


def unit_rows(values):
    floats = values.astype(jnp.float32)
    scaled = floats * lax.rsqrt(jnp.sum(floats * floats, axis=-1, keepdims=True) + epsilon)
    return scaled.astype(jnp.bfloat16)


def slot_index(owners, groups, capacity):
    onehot = (owners[:, None] == jnp.arange(groups, dtype=jnp.int32)[None, :]).astype(jnp.int32)
    earlier = jnp.cumsum(onehot, axis=0) - onehot
    ranked = jnp.sum(earlier * onehot, axis=1)
    return owners * capacity + ranked


def masked_table(scores, left_ids, right_ids, left_pos, right_pos):
    allowed = (
        (left_ids[:, None] == right_ids[None, :])
        & (right_ids[None, :] >= 0)
        & (left_pos[:, None] != right_pos[None, :])
    )
    return jnp.where(allowed, scores, jnp.float32(-1.0))


def local_general(embeddings, row_group, row_cluster):
    row_count = embeddings.shape[0]
    columns = embeddings.shape[1]
    groups = lax.axis_size("grp")
    capacity = 2 * row_count // groups
    slots_all = groups * capacity
    placed = slot_index(row_group, groups, capacity)
    normed = unit_rows(embeddings)
    outgoing = (
        jnp.zeros((slots_all, columns), jnp.bfloat16)
        .at[placed]
        .set(normed)
        .reshape(groups, capacity, columns)
    )
    out_tags = (
        jnp.full((slots_all,), -1, jnp.int32).at[placed].set(row_cluster).reshape(groups, capacity)
    )
    members, member_ids = (
        lax.all_to_all(outgoing, "grp", split_axis=0, concat_axis=0, tiled=True),
        lax.all_to_all(out_tags, "grp", split_axis=0, concat_axis=0, tiled=True),
    )
    members = members.reshape(slots_all, columns)
    member_ids = member_ids.reshape(slots_all)
    tile_here = lax.axis_index("tile")
    local_pos = jnp.arange(slots_all, dtype=jnp.int32)
    own_pos = tile_here * slots_all + local_pos
    start_best = jnp.full((slots_all,), -1.0, jnp.float32)
    piece_rows = lax.all_gather(members, "tile", axis=0, tiled=True)
    piece_ids = lax.all_gather(member_ids, "tile", axis=0, tiled=True)
    scores = jnp.einsum("id,jd->ij", members, piece_rows, preferred_element_type=jnp.float32)
    piece_pos = jnp.arange(piece_rows.shape[0], dtype=jnp.int32)
    best_sim = jnp.maximum(
        start_best, jnp.max(masked_table(scores, member_ids, piece_ids, own_pos, piece_pos), axis=1)
    )
    results = best_sim.reshape(groups, capacity)
    arrived = lax.all_to_all(results, "grp", split_axis=0, concat_axis=0, tiled=True)
    return jnp.take(arrived.reshape(slots_all), placed)


def kernel(
    x_ref, owner_ref, cluster_ref, out_ref,
    loaded, normed, send, members, tag_out, tag_in, tags, key_tags, best, result_in, picks, load_s,
    ztag_s, ztag_r, z_s, z_r, ptag_s, ptag_r, sib_s, sib_r, near_s, near_r, relay_s, relay_r, res_s, res_r,
):
    rows = x_ref.shape[0]
    groups = 4
    cap = 2 * rows // groups
    slots = groups * cap
    half = cap // 2
    early = 3 * cap
    me = lax.axis_index("grp")
    tile = lax.axis_index("tile")
    core = lax.rem(tile, 2)
    xpos = lax.rem(tile // 2, 2)
    ypos = tile // 4
    beside = 1 - 2 * core
    sib = tile + beside
    xdev = tile + 2 - 4 * xpos
    ydev = tile + 4 - 8 * ypos
    cross = 4 - xpos
    crossdev = ydev + (1 - xpos) * beside
    peer = (me, me + 1 - 2 * lax.rem(me, 2), me + 2 - 4 * (me // 2), 3 - me)

    partners = [(peer[r], tile) for r in (1, 2, 3)]
    partners += [(peer[r], device) for r in range(4) for device in (sib, xdev, ydev, ydev + beside)]
    barrier = pltpu.get_barrier_semaphore()
    for partner in partners:
        pl.semaphore_signal(barrier, inc=1, device_id=partner, device_id_type=MESH)

    load = pltpu.make_async_copy(x_ref, loaded, load_s)
    load.start()

    def remote(src, dst, ssem, rsem, device):
        return pltpu.make_async_remote_copy(
            src_ref=src, dst_ref=dst, send_sem=ssem, recv_sem=rsem, device_id=device, device_id_type=MESH
        )

    owner = owner_ref[...].reshape(1, rows)
    cluster = cluster_ref[...].reshape(1, rows)
    group_of = lax.broadcasted_iota(jnp.int32, (8, rows), 0)
    belongs = group_of == owner
    before = lax.broadcasted_iota(jnp.int32, (rows, rows), 0) < lax.broadcasted_iota(jnp.int32, (rows, rows), 1)
    earlier = jnp.dot(
        jnp.where(belongs, 1.0, 0.0).astype(jnp.bfloat16),
        jnp.where(before, 1.0, 0.0).astype(jnp.bfloat16),
        preferred_element_type=jnp.float32,
    )
    rank = jnp.sum(jnp.where(belongs, earlier, 0.0), axis=0, keepdims=True).astype(jnp.int32)
    slot = owner * cap + rank
    at_rank = jnp.where(lax.broadcasted_iota(jnp.int32, (cap, rows), 0) == rank, 1.0, 0.0).astype(jnp.bfloat16)

    load.wait()
    chunk = rows // 4
    for c in range(4):
        part = pl.ds(c * chunk, chunk)
        normed[part, :] = unit_rows(loaded[part, :])

    def filled(group):
        sel = lax.broadcasted_iota(jnp.int32, (cap, rows), 0) + group * cap
        sel = jnp.where(sel == slot, 1.0, 0.0).astype(jnp.bfloat16)
        return jnp.dot(sel, normed[...], preferred_element_type=jnp.float32).astype(jnp.bfloat16)

    def zcopy(r, p):
        part = 2 * r + p
        return remote(
            send.at[r - 1, pl.ds(p * half, half), :], members.at[0, pl.ds(part * half, half), :],
            z_s.at[part], z_r.at[part], (peer[r], tile),
        )

    def spread(r, p):
        part = 2 * r + p
        line = pl.ds(part * half, half)
        src = members.at[0, line, :]
        copies = [
            remote(src, members.at[1, line, :], sib_s.at[part], sib_r.at[part], (me, sib)),
            remote(src, members.at[2, line, :], near_s.at[0, part], near_r.at[0, part], (me, xdev)),
            remote(src, members.at[3, line, :], near_s.at[1, part], near_r.at[1, part], (me, ydev)),
        ]
        for copy in copies[::-1]:
            copy.start()
        return copies

    def relay(part, copies):
        copies[2].wait_recv()
        line = pl.ds(part * half, half)
        copy = remote(members.at[3, line, :], members.at[4, line, :], relay_s.at[part], relay_r.at[part], (me, sib))
        copy.start()
        return copy

    zcopies = {}

    def begin(r, p):
        zcopies[r, p] = zcopy(r, p)
        zcopies[r, p].start()

    send[1] = filled(peer[2])
    pl.semaphore_wait(barrier, len(partners))
    begin(2, 0)
    send[0] = filled(peer[1])
    begin(1, 0)
    members[0, 0:cap, :] = filled(me)
    spreads, relays = [spread(0, 0), spread(0, 1)], []
    send[2] = filled(peer[3])

    marks = jnp.where(belongs, (cluster + 1).astype(jnp.float32), 0.0).astype(jnp.bfloat16)
    marked = lax.dot_general(marks, at_rank, NT, preferred_element_type=jnp.float32)
    tag_out[...] = jnp.zeros(tag_out.shape, jnp.float32)
    ztags = []
    for r in range(4):
        tag_out[r, :, r * cap : (r + 1) * cap] = marked
        if r:
            copy = remote(tag_out.at[r], tag_in.at[r - 1], ztag_s.at[r - 1], ztag_r.at[r - 1], (peer[r], tile))
            copy.start()
            ztags.append(copy)

    zcopies[2, 0].wait_send()
    begin(2, 1)
    zcopies[1, 0].wait_send()
    begin(1, 1)

    for copy in ztags:
        copy.wait_recv()
    total = tag_out[0] + tag_in[0] + tag_in[1] + tag_in[2]
    tags[0] = jnp.sum(
        jnp.where(lax.broadcasted_iota(jnp.int32, (8, slots), 0) == me, total, 0.0), axis=0, keepdims=True
    )
    ptags = []
    for n, device in enumerate((sib, xdev, ydev, ydev + beside)):
        copy = remote(tags.at[0], tags.at[1 + n], ptag_s.at[n], ptag_r.at[n], (me, device))
        copy.start()
        ptags.append(copy)

    zcopies[1, 0].wait_recv()
    spreads.append(spread(1, 0))
    zcopies[2, 0].wait_recv()
    spreads.append(spread(2, 0))
    zcopies[2, 1].wait_send()
    begin(3, 0)
    zcopies[1, 1].wait_recv()
    spreads.append(spread(1, 1))
    zcopies[2, 1].wait_recv()
    spreads.append(spread(2, 1))
    parts = [0, 1, 2, 4, 3, 5, 6, 7]

    for copy in ptags:
        copy.wait_recv()
    best[...] = jnp.full(best.shape, -1.0, jnp.float32)
    for n in range(5):
        for i in range(groups):
            first = i * cap // 128 * 128
            lanes = lax.broadcasted_iota(jnp.int32, (cap, 256), 1) + (first - i * cap)
            wanted = lax.broadcasted_iota(jnp.int32, (cap, 256), 0)
            picked = jnp.sum(
                jnp.where(lanes == wanted, tags[n, :, first : first + 256], 0.0), axis=1, keepdims=True
            )
            picked = jnp.where(picked > 0.0, picked, -1.0)
            key_tags[n, i * cap : (i + 1) * cap, :] = jnp.broadcast_to(picked, (cap, 128))

    def compare(kblock, keys, qblock, queries, to, own=False):
        (k0, k1), (q0, q1) = keys, queries
        shape = (k1 - k0, q1 - q0)
        scores = lax.dot_general(
            members[kblock, k0:k1, :], members[qblock, q0:q1, :], NT, preferred_element_type=jnp.float32
        )
        allowed = key_tags[kblock, k0:k1, 0:1] == tags[qblock, :, q0:q1]
        if own:
            line = lax.broadcasted_iota(jnp.int32, shape, 0) + (k0 + (kblock + qblock) * 2 * slots)
            lane = lax.broadcasted_iota(jnp.int32, shape, 1) + q0
            allowed = allowed & (line != lane)
        found = jnp.max(jnp.where(allowed, scores, -1.0), axis=0, keepdims=True)
        best[to, :, q0:q1] = jnp.maximum(best[to, :, q0:q1], found)

    first, last, whole = (0, early), (early, slots), (0, slots)

    for n in (0, 1, 2):
        relays.append(relay(parts[n], spreads[n]))
    zcopies[3, 0].wait_send()
    begin(3, 1)
    for n in (3, 4, 5):
        relays.append(relay(parts[n], spreads[n]))
    zcopies[3, 0].wait_recv()
    spreads.append(spread(3, 0))
    for copies in spreads[:6]:
        copies[0].wait_recv()
        copies[1].wait_recv()

    @pl.loop(0, 6)
    def _(i):
        j = i // 2
        q = lax.rem(i, 2)
        compare(j + (j + 1) // 2, first, q, first, q, own=True)

    zcopies[3, 1].wait_recv()
    spreads.append(spread(3, 1))
    for copy in relays[:6]:
        copy.wait_recv()

    @pl.loop(0, 2)
    def _(q):
        compare(cross + q * (2 - cross), first, 2 + q * (cross - 2), first, 2 + q)

    relays.append(relay(parts[6], spreads[6]))
    for copies in spreads[6:]:
        copies[0].wait_recv()

    @pl.loop(0, 6)
    def _(i):
        j = i // 2
        q = lax.rem(i, 2)
        compare(j + (j + 1) // 2, first, q, last, q, own=True)

    @pl.loop(0, 2)
    def _(q):
        compare(0, last, q, whole, q, own=True)

    relays.append(relay(parts[7], spreads[7]))
    for copies in spreads[6:]:
        copies[1].wait_recv()

    @pl.loop(0, 4)
    def _(i):
        q = lax.rem(i, 2)
        compare(2 + i // 2, last, q, whole, q)

    for copy in relays[6:]:
        copy.wait_recv()

    @pl.loop(0, 2)
    def _(q):
        compare(cross + q * (2 - cross), first, 2 + q * (cross - 2), last, 2 + q)

    @pl.loop(0, 2)
    def _(q):
        compare(cross + q * (2 - cross), last, 2 + q * (cross - 2), whole, 2 + q)

    copies = []
    for h, device in enumerate((tile, sib, xdev, crossdev)):
        for r in (3, 2, 1, 0):
            index = h * 4 + r
            if index == 0:
                result_in[0] = best[0]
                continue
            copy = remote(
                best.at[h], result_in.at[index], res_s.at[index], res_r.at[index], (peer[r], device)
            )
            copy.start()
            copies.append(copy)
    for copy in copies:
        copy.wait_recv()

    picks[...] = jnp.zeros(picks.shape, jnp.float32)
    for r in range(4):
        block = jnp.maximum(
            jnp.maximum(result_in[r], result_in[4 + r]), jnp.maximum(result_in[8 + r], result_in[12 + r])
        )[:, r * cap : (r + 1) * cap]
        high = block.astype(jnp.bfloat16).astype(jnp.float32)
        middle = (block - high).astype(jnp.bfloat16).astype(jnp.float32)
        picks[r : r + 1, :] = high
        picks[4 + r : 5 + r, :] = middle
        picks[8 + r : 9 + r, :] = (block - high) - middle
    found = jnp.dot(picks[...].astype(jnp.bfloat16), at_rank, preferred_element_type=jnp.float32)
    out = jnp.zeros((1, rows), jnp.float32)
    for r in range(4):
        value = (found[r : r + 1, :] + found[4 + r : 5 + r, :]) + found[8 + r : 9 + r, :]
        out = jnp.where(owner == peer[r], value, out)
    out_ref[...] = out.reshape(rows)

    for copy in ztags + ptags + copies + relays + [zcopies[1, 1], zcopies[3, 1]]:
        copy.wait_send()
    for group in spreads:
        for copy in group:
            copy.wait_send()


def local_fused(embeddings, row_group, row_cluster):
    rows, columns = embeddings.shape
    slots = 2 * rows
    dma = pltpu.SemaphoreType.DMA
    return pl.pallas_call(
        kernel,
        out_shape=jax.ShapeDtypeStruct((rows,), jnp.float32),
        in_specs=[pl.BlockSpec(memory_space=pl.ANY)] + [pl.BlockSpec(memory_space=pltpu.VMEM)] * 2,
        out_specs=pl.BlockSpec(memory_space=pltpu.VMEM),
        scratch_shapes=[
            pltpu.VMEM((rows, columns), jnp.bfloat16),
            pltpu.VMEM((rows, columns), jnp.bfloat16),
            pltpu.VMEM((3, slots // 4, columns), jnp.bfloat16),
            pltpu.VMEM((5, slots, columns), jnp.bfloat16),
            pltpu.VMEM((4, 8, slots), jnp.float32),
            pltpu.VMEM((3, 8, slots), jnp.float32),
            pltpu.VMEM((5, 1, slots), jnp.float32),
            pltpu.VMEM((5, slots, 128), jnp.float32),
            pltpu.VMEM((4, 1, slots), jnp.float32),
            pltpu.VMEM((16, 1, slots), jnp.float32),
            pltpu.VMEM((16, slots // 4), jnp.float32),
            dma(()),
            dma((3,)), dma((3,)), dma((8,)), dma((8,)),
            dma((4,)), dma((4,)), dma((8,)), dma((8,)),
            dma((2, 8)), dma((2, 8)), dma((8,)), dma((8,)),
            dma((16,)), dma((16,)),
        ],
        compiler_params=pltpu.CompilerParams(
            collective_id=0, has_side_effects=True, vmem_limit_bytes=48 * 1024 * 1024
        ),
    )(embeddings, row_group, row_cluster)


def solution(mesh):
    fused = mesh.shape["grp"] == 4 and mesh.shape["tile"] == 8
    placed = (P(("grp", "tile"), None), P(("grp", "tile")), P(("grp", "tile")))
    return jax.shard_map(
        local_fused if fused else local_general,
        mesh=mesh, in_specs=placed, out_specs=P(("grp", "tile")), check_vma=False,
    )
```

time: 69.9 us -> 69.8 us (level)
  local copies, waits for them, and re-layouts: 1.83 us -> 3.08 us
  Pallas kernels: 67.2 us -> 66.5 us
    unnamed x4 -> x7, local copies, waits for them, and re-layouts: 1.13 us -> 3.08 us
    pallas_call x1, Pallas kernels: 67.2 us -> 66.5 us  [local_fused(): pl.pallas_call(kernel, out_shape=jax.ShapeDtypeStruct((rows,), jnp.float3...]
where the time goes in v4:
time: 69.8 us; the launch traced here: 69.6 us
  Pallas kernels  66.5 us (95%)
  local copies, waits for them, and re-layouts  3.08 us (4%)
    pallas_call x1, Pallas kernels, local_fused(): pl.pallas_call(kernel, out_shape=jax.ShapeDtypeStruct((rows,), jnp.float3...  66.5 us
    unnamed x7, local copies, waits for them, and re-layouts  3.08 us

profile of v4, /device:TPU:0, one launch (start us, length us, event | category | flops | bytes accessed | tf_op | source)
XLA Modules:
  0.0 69.6 jit_solution(9952109622205979315)
XLA Ops:
  0.0 0.0 copy-start
  0.0 1.1 %copy-done = bf16[384,1024]{1,0:T(8,128)(2,1)S(1)} copy-done((bf16[384,1024]{1,0:T(8,128)(2,1)S(1)}, bf16[384,1024]{1,0:T(8,128)(2,1)}, u32[]{:S(2)}) %copy-start) | copy-done | bytes 786456
  1.1 0.0 copy-start.1
  1.1 0.7 copy-done.1
  1.8 0.0 copy-start.2
  1.8 0.7 copy-done.2
  2.5 66.5 %shard_map.37 = f32[384]{0:T(512)S(1)} custom-call(bf16[384,1024]{1,0:T(8,128)(2,1)S(1)} %copy-done, s32[384]{0:T(512)S(1)} %copy-done.1, s32[384]{0:T(512)S(1)} %copy-done.2), custom_call_target="tpu_custom_call" | custom-call | tf_op jit(solution)/shard_map/pallas_call | solution.py:353
  69.0 0.6 copy.5
Async XLA Ops:
  0.0 1.1 %copy-start = (bf16[384,1024]{1,0:T(8,128)(2,1)S(1)}, bf16[384,1024]{1,0:T(8,128)(2,1)}, u32[]{:S(2)}) copy-start(bf16[384,1024]{1,0:T(8,128)(2,1)} %x_ref.1) | copy-start | bytes 2359300
  1.1 0.7 copy-start.1
  1.8 0.7 copy-start.2

commit v5 on v4

--- a/solution.py
+++ b/solution.py
@@ -73,7 +73,7 @@
 
 def kernel(
     x_ref, owner_ref, cluster_ref, out_ref,
-    loaded, normed, send, members, tag_out, tag_in, tags, key_tags, best, result_in, picks, load_s,
+    loaded, owners, clusters, normed, send, members, tag_out, tag_in, tags, key_tags, best, result_in, picks, load_s,
     ztag_s, ztag_r, z_s, z_r, ptag_s, ptag_r, sib_s, sib_r, near_s, near_r, relay_s, relay_r, res_s, res_r,
 ):
     rows = x_ref.shape[0]
@@ -101,16 +101,22 @@
     for partner in partners:
         pl.semaphore_signal(barrier, inc=1, device_id=partner, device_id_type=MESH)
 
-    load = pltpu.make_async_copy(x_ref, loaded, load_s)
-    load.start()
+    loads = [
+        pltpu.make_async_copy(src, dst, load_s.at[n])
+        for n, (src, dst) in enumerate(((owner_ref, owners), (cluster_ref, clusters), (x_ref, loaded)))
+    ]
+    for load in loads:
+        load.start()
 
     def remote(src, dst, ssem, rsem, device):
         return pltpu.make_async_remote_copy(
             src_ref=src, dst_ref=dst, send_sem=ssem, recv_sem=rsem, device_id=device, device_id_type=MESH
         )
 
-    owner = owner_ref[...].reshape(1, rows)
-    cluster = cluster_ref[...].reshape(1, rows)
+    loads[0].wait()
+    loads[1].wait()
+    owner = owners[...].reshape(1, rows)
+    cluster = clusters[...].reshape(1, rows)
     group_of = lax.broadcasted_iota(jnp.int32, (8, rows), 0)
     belongs = group_of == owner
     before = lax.broadcasted_iota(jnp.int32, (rows, rows), 0) < lax.broadcasted_iota(jnp.int32, (rows, rows), 1)
@@ -123,7 +129,7 @@
     slot = owner * cap + rank
     at_rank = jnp.where(lax.broadcasted_iota(jnp.int32, (cap, rows), 0) == rank, 1.0, 0.0).astype(jnp.bfloat16)
 
-    load.wait()
+    loads[2].wait()
     chunk = rows // 4
     for c in range(4):
         part = pl.ds(c * chunk, chunk)
@@ -170,8 +176,10 @@
     send[1] = filled(peer[2])
     pl.semaphore_wait(barrier, len(partners))
     begin(2, 0)
+    begin(2, 1)
     send[0] = filled(peer[1])
     begin(1, 0)
+    begin(1, 1)
     members[0, 0:cap, :] = filled(me)
     spreads, relays = [spread(0, 0), spread(0, 1)], []
     send[2] = filled(peer[3])
@@ -187,11 +195,6 @@
             copy.start()
             ztags.append(copy)
 
-    zcopies[2, 0].wait_send()
-    begin(2, 1)
-    zcopies[1, 0].wait_send()
-    begin(1, 1)
-
     for copy in ztags:
         copy.wait_recv()
     total = tag_out[0] + tag_in[0] + tag_in[1] + tag_in[2]
@@ -206,12 +209,14 @@
 
     zcopies[1, 0].wait_recv()
     spreads.append(spread(1, 0))
+    zcopies[2, 0].wait_send()
+    begin(3, 0)
     zcopies[2, 0].wait_recv()
     spreads.append(spread(2, 0))
-    zcopies[2, 1].wait_send()
-    begin(3, 0)
     zcopies[1, 1].wait_recv()
     spreads.append(spread(1, 1))
+    zcopies[2, 1].wait_send()
+    begin(3, 1)
     zcopies[2, 1].wait_recv()
     spreads.append(spread(2, 1))
     parts = [0, 1, 2, 4, 3, 5, 6, 7]
@@ -246,23 +251,26 @@
 
     first, last, whole = (0, early), (early, slots), (0, slots)
 
-    for n in (0, 1, 2):
-        relays.append(relay(parts[n], spreads[n]))
-    zcopies[3, 0].wait_send()
-    begin(3, 1)
-    for n in (3, 4, 5):
+    for copies in spreads[:6]:
+        copies[0].wait_recv()
+
+    @pl.loop(0, 2)
+    def _(q):
+        compare(0, first, q, first, q, own=True)
+
+    for n in (0, 1, 2, 3):
         relays.append(relay(parts[n], spreads[n]))
     zcopies[3, 0].wait_recv()
     spreads.append(spread(3, 0))
+    for n in (4, 5):
+        relays.append(relay(parts[n], spreads[n]))
     for copies in spreads[:6]:
-        copies[0].wait_recv()
         copies[1].wait_recv()
 
-    @pl.loop(0, 6)
+    @pl.loop(0, 4)
     def _(i):
-        j = i // 2
         q = lax.rem(i, 2)
-        compare(j + (j + 1) // 2, first, q, first, q, own=True)
+        compare(2 + i // 2, first, q, first, q)
 
     zcopies[3, 1].wait_recv()
     spreads.append(spread(3, 1))
@@ -339,7 +347,7 @@
         out = jnp.where(owner == peer[r], value, out)
     out_ref[...] = out.reshape(rows)
 
-    for copy in ztags + ptags + copies + relays + [zcopies[1, 1], zcopies[3, 1]]:
+    for copy in ztags + ptags + copies + relays + [zcopies[1, 0], zcopies[1, 1], zcopies[3, 0], zcopies[3, 1]]:
         copy.wait_send()
     for group in spreads:
         for copy in group:
@@ -353,10 +361,12 @@
     return pl.pallas_call(
         kernel,
         out_shape=jax.ShapeDtypeStruct((rows,), jnp.float32),
-        in_specs=[pl.BlockSpec(memory_space=pl.ANY)] + [pl.BlockSpec(memory_space=pltpu.VMEM)] * 2,
+        in_specs=[pl.BlockSpec(memory_space=pltpu.HBM)] * 3,
         out_specs=pl.BlockSpec(memory_space=pltpu.VMEM),
         scratch_shapes=[
             pltpu.VMEM((rows, columns), jnp.bfloat16),
+            pltpu.VMEM((rows,), jnp.int32),
+            pltpu.VMEM((rows,), jnp.int32),
             pltpu.VMEM((rows, columns), jnp.bfloat16),
             pltpu.VMEM((3, slots // 4, columns), jnp.bfloat16),
             pltpu.VMEM((5, slots, columns), jnp.bfloat16),
@@ -367,7 +377,7 @@
             pltpu.VMEM((4, 1, slots), jnp.float32),
             pltpu.VMEM((16, 1, slots), jnp.float32),
             pltpu.VMEM((16, slots // 4), jnp.float32),
-            dma(()),
+            dma((3,)),
             dma((3,)), dma((3,)), dma((8,)), dma((8,)),
             dma((4,)), dma((4,)), dma((8,)), dma((8,)),
             dma((2, 8)), dma((2, 8)), dma((8,)), dma((8,)),

time: 69.8 us -> 73.4 us (1.052)
  Pallas kernels: 66.5 us -> 70.1 us
    pallas_call x1, Pallas kernels: 66.5 us -> 70.1 us  [local_fused(): pl.pallas_call(kernel, out_shape=jax.ShapeDtypeStruct((rows,), jnp.float3...]
where the time goes in v5:
time: 73.4 us; the launch traced here: 73.2 us
  Pallas kernels  70.1 us (96%)
  local copies, waits for them, and re-layouts  3.08 us (4%)
    pallas_call x1, Pallas kernels, local_fused(): pl.pallas_call(kernel, out_shape=jax.ShapeDtypeStruct((rows,), jnp.float3...  70.1 us
    unnamed x7, local copies, waits for them, and re-layouts  3.08 us

profile of v5, /device:TPU:0, one launch (start us, length us, event | category | flops | bytes accessed | tf_op | source)
XLA Modules:
  0.0 73.2 jit_solution(18347747000026272823)
XLA Ops:
  0.0 0.0 copy-start
  0.0 1.1 %copy-done = bf16[384,1024]{1,0:T(8,128)(2,1)S(1)} copy-done((bf16[384,1024]{1,0:T(8,128)(2,1)S(1)}, bf16[384,1024]{1,0:T(8,128)(2,1)}, u32[]{:S(2)}) %copy-start) | copy-done | bytes 786456
  1.1 0.0 copy-start.1
  1.1 0.7 copy-done.1
  1.8 0.0 copy-start.2
  1.8 0.7 copy-done.2
  2.5 70.1 %shard_map.37 = f32[384]{0:T(512)S(1)} custom-call(bf16[384,1024]{1,0:T(8,128)(2,1)S(1)} %copy-done, s32[384]{0:T(512)S(1)} %copy-done.1, s32[384]{0:T(512)S(1)} %copy-done.2), custom_call_target="tpu_custom_call" | custom-call | tf_op jit(solution)/shard_map/pallas_call | solution.py:361
  72.7 0.6 copy.5
Async XLA Ops:
  0.0 1.1 %copy-start = (bf16[384,1024]{1,0:T(8,128)(2,1)S(1)}, bf16[384,1024]{1,0:T(8,128)(2,1)}, u32[]{:S(2)}) copy-start(bf16[384,1024]{1,0:T(8,128)(2,1)} %x_ref.1) | copy-start | bytes 2359300
  1.1 0.7 copy-start.1
  1.8 0.7 copy-start.2

commit v6 on v5

--- a/solution.py
+++ b/solution.py
@@ -164,8 +164,18 @@
         copies[2].wait_recv()
         line = pl.ds(part * half, half)
         copy = remote(members.at[3, line, :], members.at[4, line, :], relay_s.at[part], relay_r.at[part], (me, sib))
-        copy.start()
+
+        @pl.when(xpos == 0)
+        def _():
+            copy.start()
+
         return copy
+
+    def relayed(copies, wait):
+        @pl.when(xpos == 0)
+        def _():
+            for copy in copies:
+                wait(copy)
 
     zcopies = {}
 
@@ -176,10 +186,8 @@
     send[1] = filled(peer[2])
     pl.semaphore_wait(barrier, len(partners))
     begin(2, 0)
-    begin(2, 1)
     send[0] = filled(peer[1])
     begin(1, 0)
-    begin(1, 1)
     members[0, 0:cap, :] = filled(me)
     spreads, relays = [spread(0, 0), spread(0, 1)], []
     send[2] = filled(peer[3])
@@ -195,6 +203,11 @@
             copy.start()
             ztags.append(copy)
 
+    zcopies[2, 0].wait_send()
+    begin(2, 1)
+    zcopies[1, 0].wait_send()
+    begin(1, 1)
+
     for copy in ztags:
         copy.wait_recv()
     total = tag_out[0] + tag_in[0] + tag_in[1] + tag_in[2]
@@ -209,14 +222,12 @@
 
     zcopies[1, 0].wait_recv()
     spreads.append(spread(1, 0))
-    zcopies[2, 0].wait_send()
-    begin(3, 0)
     zcopies[2, 0].wait_recv()
     spreads.append(spread(2, 0))
+    zcopies[2, 1].wait_send()
+    begin(3, 0)
     zcopies[1, 1].wait_recv()
     spreads.append(spread(1, 1))
-    zcopies[2, 1].wait_send()
-    begin(3, 1)
     zcopies[2, 1].wait_recv()
     spreads.append(spread(2, 1))
     parts = [0, 1, 2, 4, 3, 5, 6, 7]
@@ -258,6 +269,8 @@
     def _(q):
         compare(0, first, q, first, q, own=True)
 
+    zcopies[3, 0].wait_send()
+    begin(3, 1)
     for n in (0, 1, 2, 3):
         relays.append(relay(parts[n], spreads[n]))
     zcopies[3, 0].wait_recv()
@@ -274,8 +287,7 @@
 
     zcopies[3, 1].wait_recv()
     spreads.append(spread(3, 1))
-    for copy in relays[:6]:
-        copy.wait_recv()
+    relayed(relays[:6], lambda copy: copy.wait_recv())
 
     @pl.loop(0, 2)
     def _(q):
@@ -304,8 +316,7 @@
         q = lax.rem(i, 2)
         compare(2 + i // 2, last, q, whole, q)
 
-    for copy in relays[6:]:
-        copy.wait_recv()
+    relayed(relays[6:], lambda copy: copy.wait_recv())
 
     @pl.loop(0, 2)
     def _(q):
@@ -347,11 +358,12 @@
         out = jnp.where(owner == peer[r], value, out)
     out_ref[...] = out.reshape(rows)
 
-    for copy in ztags + ptags + copies + relays + [zcopies[1, 0], zcopies[1, 1], zcopies[3, 0], zcopies[3, 1]]:
+    for copy in ztags + ptags + copies + [zcopies[1, 1], zcopies[3, 1]]:
         copy.wait_send()
     for group in spreads:
         for copy in group:
             copy.wait_send()
+    relayed(relays, lambda copy: copy.wait_send())
 
 
 def local_fused(embeddings, row_group, row_cluster):
@@ -384,7 +396,7 @@
             dma((16,)), dma((16,)),
         ],
         compiler_params=pltpu.CompilerParams(
-            collective_id=0, has_side_effects=True, vmem_limit_bytes=48 * 1024 * 1024
+            collective_id=0, has_side_effects=True, vmem_limit_bytes=64 * 1024 * 1024 - 256 * 1024
         ),
     )(embeddings, row_group, row_cluster)
 

time: 73.4 us -> 65.3 us (0.89)
  Pallas kernels: 70.1 us -> 63.8 us
  local copies, waits for them, and re-layouts: 3.08 us -> 1.26 us
    pallas_call x1, Pallas kernels: 70.1 us -> 63.8 us  [local_fused(): pl.pallas_call(kernel, out_shape=jax.ShapeDtypeStruct((rows,), jnp.float3...]
    unnamed x7 -> x1, local copies, waits for them, and re-layouts: 3.08 us -> 1.26 us
where the time goes in v6:
time: 65.3 us; the launch traced here: 65.1 us
  Pallas kernels  63.8 us (98%)
  local copies, waits for them, and re-layouts  1.26 us (2%)
    pallas_call x1, Pallas kernels, local_fused(): pl.pallas_call(kernel, out_shape=jax.ShapeDtypeStruct((rows,), jnp.float3...  63.8 us

profile of v6, /device:TPU:0, one launch (start us, length us, event | category | flops | bytes accessed | tf_op | source)
XLA Modules:
  0.0 65.1 jit_solution(4992998950881361858)
XLA Ops:
  0.0 63.8 %shard_map.37 = f32[384]{0:T(512)} custom-call(bf16[384,1024]{1,0:T(8,128)(2,1)} %x_ref.1, s32[384]{0:T(512)} %owner_ref.1, s32[384]{0:T(512)} %cluster_ref.1), custom_call_target="tpu_custom_call" | custom-call | tf_op jit(solution)/shard_map/pallas_call | solution.py:373
  63.8 1.3 %copy.5 = f32[384]{0:T(512)} copy(f32[384]{0:T(512)} %shard_map.37) | data formatting | bytes 3072

commit v7 on v6

--- a/solution.py
+++ b/solution.py
@@ -140,16 +140,27 @@
         sel = jnp.where(sel == slot, 1.0, 0.0).astype(jnp.bfloat16)
         return jnp.dot(sel, normed[...], preferred_element_type=jnp.float32).astype(jnp.bfloat16)
 
-    def zcopy(r, p):
-        part = 2 * r + p
-        return remote(
-            send.at[r - 1, pl.ds(p * half, half), :], members.at[0, pl.ds(part * half, half), :],
+    sixth = cap // 6
+    parts = ((0, 0, 6), (1, 0, 3), (1, 3, 6), (2, 0, 1), (2, 1, 3), (2, 3, 6), (3, 0, 3), (3, 3, 6))
+
+    def begin(part):
+        r, low, high = parts[part]
+        copy = remote(
+            send.at[r - 1, pl.ds(low * sixth, (high - low) * sixth), :],
+            members.at[0, pl.ds(r * cap + low * sixth, (high - low) * sixth), :],
             z_s.at[part], z_r.at[part], (peer[r], tile),
         )
-
-    def spread(r, p):
-        part = 2 * r + p
-        line = pl.ds(part * half, half)
+        copy.start()
+        zcopies[part] = copy
+
+    def line_of(part):
+        r, low, high = parts[part]
+        return pl.ds(r * cap + low * sixth, (high - low) * sixth)
+
+    def spread(part):
+        if part:
+            zcopies[part].wait_recv()
+        line = line_of(part)
         src = members.at[0, line, :]
         copies = [
             remote(src, members.at[1, line, :], sib_s.at[part], sib_r.at[part], (me, sib)),
@@ -158,18 +169,18 @@
         ]
         for copy in copies[::-1]:
             copy.start()
-        return copies
-
-    def relay(part, copies):
-        copies[2].wait_recv()
-        line = pl.ds(part * half, half)
+        spreads[part] = copies
+
+    def relay(part):
+        spreads[part][2].wait_recv()
+        line = line_of(part)
         copy = remote(members.at[3, line, :], members.at[4, line, :], relay_s.at[part], relay_r.at[part], (me, sib))
 
         @pl.when(xpos == 0)
         def _():
             copy.start()
 
-        return copy
+        relays[part] = copy
 
     def relayed(copies, wait):
         @pl.when(xpos == 0)
@@ -177,19 +188,15 @@
             for copy in copies:
                 wait(copy)
 
-    zcopies = {}
-
-    def begin(r, p):
-        zcopies[r, p] = zcopy(r, p)
-        zcopies[r, p].start()
-
+    zcopies, spreads, relays = {}, {}, {}
     send[1] = filled(peer[2])
     pl.semaphore_wait(barrier, len(partners))
-    begin(2, 0)
+    begin(3)
+    begin(4)
     send[0] = filled(peer[1])
-    begin(1, 0)
+    begin(1)
     members[0, 0:cap, :] = filled(me)
-    spreads, relays = [spread(0, 0), spread(0, 1)], []
+    spread(0)
     send[2] = filled(peer[3])
 
     marks = jnp.where(belongs, (cluster + 1).astype(jnp.float32), 0.0).astype(jnp.bfloat16)
@@ -203,10 +210,15 @@
             copy.start()
             ztags.append(copy)
 
-    zcopies[2, 0].wait_send()
-    begin(2, 1)
-    zcopies[1, 0].wait_send()
-    begin(1, 1)
+    zcopies[3].wait_send()
+    begin(5)
+    spread(3)
+    zcopies[1].wait_send()
+    begin(2)
+    spread(1)
+    zcopies[4].wait_send()
+    begin(6)
+    spread(4)
 
     for copy in ztags:
         copy.wait_recv()
@@ -219,18 +231,6 @@
         copy = remote(tags.at[0], tags.at[1 + n], ptag_s.at[n], ptag_r.at[n], (me, device))
         copy.start()
         ptags.append(copy)
-
-    zcopies[1, 0].wait_recv()
-    spreads.append(spread(1, 0))
-    zcopies[2, 0].wait_recv()
-    spreads.append(spread(2, 0))
-    zcopies[2, 1].wait_send()
-    begin(3, 0)
-    zcopies[1, 1].wait_recv()
-    spreads.append(spread(1, 1))
-    zcopies[2, 1].wait_recv()
-    spreads.append(spread(2, 1))
-    parts = [0, 1, 2, 4, 3, 5, 6, 7]
 
     for copy in ptags:
         copy.wait_recv()
@@ -262,40 +262,39 @@
 
     first, last, whole = (0, early), (early, slots), (0, slots)
 
-    for copies in spreads[:6]:
-        copies[0].wait_recv()
+    spread(2)
+    zcopies[5].wait_send()
+    begin(7)
+    spread(5)
+    for part in range(6):
+        spreads[part][0].wait_recv()
 
     @pl.loop(0, 2)
     def _(q):
         compare(0, first, q, first, q, own=True)
 
-    zcopies[3, 0].wait_send()
-    begin(3, 1)
-    for n in (0, 1, 2, 3):
-        relays.append(relay(parts[n], spreads[n]))
-    zcopies[3, 0].wait_recv()
-    spreads.append(spread(3, 0))
-    for n in (4, 5):
-        relays.append(relay(parts[n], spreads[n]))
-    for copies in spreads[:6]:
-        copies[1].wait_recv()
+    for part in (0, 3, 1, 4, 2):
+        relay(part)
+    spread(6)
+    relay(5)
+    for part in range(6):
+        spreads[part][1].wait_recv()
 
     @pl.loop(0, 4)
     def _(i):
         q = lax.rem(i, 2)
         compare(2 + i // 2, first, q, first, q)
 
-    zcopies[3, 1].wait_recv()
-    spreads.append(spread(3, 1))
-    relayed(relays[:6], lambda copy: copy.wait_recv())
+    spread(7)
+    relayed([relays[part] for part in range(6)], lambda copy: copy.wait_recv())
 
     @pl.loop(0, 2)
     def _(q):
         compare(cross + q * (2 - cross), first, 2 + q * (cross - 2), first, 2 + q)
 
-    relays.append(relay(parts[6], spreads[6]))
-    for copies in spreads[6:]:
-        copies[0].wait_recv()
+    relay(6)
+    for part in (6, 7):
+        spreads[part][0].wait_recv()
 
     @pl.loop(0, 6)
     def _(i):
@@ -307,16 +306,16 @@
     def _(q):
         compare(0, last, q, whole, q, own=True)
 
-    relays.append(relay(parts[7], spreads[7]))
-    for copies in spreads[6:]:
-        copies[1].wait_recv()
+    relay(7)
+    for part in (6, 7):
+        spreads[part][1].wait_recv()
 
     @pl.loop(0, 4)
     def _(i):
         q = lax.rem(i, 2)
         compare(2 + i // 2, last, q, whole, q)
 
-    relayed(relays[6:], lambda copy: copy.wait_recv())
+    relayed([relays[6], relays[7]], lambda copy: copy.wait_recv())
 
     @pl.loop(0, 2)
     def _(q):
@@ -358,12 +357,12 @@
         out = jnp.where(owner == peer[r], value, out)
     out_ref[...] = out.reshape(rows)
 
-    for copy in ztags + ptags + copies + [zcopies[1, 1], zcopies[3, 1]]:
+    for copy in ztags + ptags + copies + [zcopies[2], zcopies[6], zcopies[7]]:
         copy.wait_send()
-    for group in spreads:
+    for group in spreads.values():
         for copy in group:
             copy.wait_send()
-    relayed(relays, lambda copy: copy.wait_send())
+    relayed(list(relays.values()), lambda copy: copy.wait_send())
 
 
 def local_fused(embeddings, row_group, row_cluster):

time: 65.3 us -> 65.5 us (level)
  no operation moved by 1% of the time
where the time goes in v7:
time: 65.5 us; the launch traced here: 65.4 us
  Pallas kernels  64.1 us (98%)
  local copies, waits for them, and re-layouts  1.26 us (2%)
    pallas_call x1, Pallas kernels, local_fused(): pl.pallas_call(kernel, out_shape=jax.ShapeDtypeStruct((rows,), jnp.float3...  64.1 us

profile of v7, /device:TPU:0, one launch (start us, length us, event | category | flops | bytes accessed | tf_op | source)
XLA Modules:
  0.0 65.4 jit_solution(3744360110536501149)
XLA Ops:
  0.0 64.1 %shard_map.37 = f32[384]{0:T(512)} custom-call(bf16[384,1024]{1,0:T(8,128)(2,1)} %x_ref.1, s32[384]{0:T(512)} %owner_ref.1, s32[384]{0:T(512)} %cluster_ref.1), custom_call_target="tpu_custom_call" | custom-call | tf_op jit(solution)/shard_map/pallas_call | solution.py:372
  64.1 1.3 %copy.5 = f32[384]{0:T(512)} copy(f32[384]{0:T(512)} %shard_map.37) | data formatting | bytes 3072

commit v8 on v7

--- a/solution.py
+++ b/solution.py
@@ -73,7 +73,7 @@
 
 def kernel(
     x_ref, owner_ref, cluster_ref, out_ref,
-    loaded, owners, clusters, normed, send, members, tag_out, tag_in, tags, key_tags, best, result_in, picks, load_s,
+    loaded, owners, clusters, normed, send, members, tag_out, tag_in, tags, key_tags, best, key_best, result_in, picks, load_s,
     ztag_s, ztag_r, z_s, z_r, ptag_s, ptag_r, sib_s, sib_r, near_s, near_r, relay_s, relay_r, res_s, res_r,
 ):
     rows = x_ref.shape[0]
@@ -235,6 +235,7 @@
     for copy in ptags:
         copy.wait_recv()
     best[...] = jnp.full(best.shape, -1.0, jnp.float32)
+    key_best[...] = jnp.full(key_best.shape, -1.0, jnp.float32)
     for n in range(5):
         for i in range(groups):
             first = i * cap // 128 * 128
@@ -246,7 +247,7 @@
             picked = jnp.where(picked > 0.0, picked, -1.0)
             key_tags[n, i * cap : (i + 1) * cap, :] = jnp.broadcast_to(picked, (cap, 128))
 
-    def compare(kblock, keys, qblock, queries, to, own=False):
+    def compare(kblock, keys, qblock, queries, to, own=False, back=None):
         (k0, k1), (q0, q1) = keys, queries
         shape = (k1 - k0, q1 - q0)
         scores = lax.dot_general(
@@ -257,8 +258,18 @@
             line = lax.broadcasted_iota(jnp.int32, shape, 0) + (k0 + (kblock + qblock) * 2 * slots)
             lane = lax.broadcasted_iota(jnp.int32, shape, 1) + q0
             allowed = allowed & (line != lane)
-        found = jnp.max(jnp.where(allowed, scores, -1.0), axis=0, keepdims=True)
+        masked = jnp.where(allowed, scores, -1.0)
+        found = jnp.max(masked, axis=0, keepdims=True)
         best[to, :, q0:q1] = jnp.maximum(best[to, :, q0:q1], found)
+        if back is not None:
+            full = shape[1] // 128 * 128
+            across = key_best[back, k0:k1, :]
+            for lane in range(0, full, 128):
+                across = jnp.maximum(across, masked[:, lane : lane + 128])
+            key_best[back, k0:k1, :] = across
+            rest = shape[1] - full
+            if rest:
+                key_best[back, k0:k1, :rest] = jnp.maximum(key_best[back, k0:k1, :rest], masked[:, full:])
 
     first, last, whole = (0, early), (early, slots), (0, slots)
 
@@ -280,27 +291,29 @@
     for part in range(6):
         spreads[part][1].wait_recv()
 
-    @pl.loop(0, 4)
+    def beside_block(i):
+        return xpos + i * (ypos - xpos)
+
+    @pl.loop(0, 2)
     def _(i):
-        q = lax.rem(i, 2)
-        compare(2 + i // 2, first, q, first, q)
+        compare(2 + i, first, beside_block(i), first, beside_block(i), back=i)
 
     spread(7)
     relayed([relays[part] for part in range(6)], lambda copy: copy.wait_recv())
 
-    @pl.loop(0, 2)
-    def _(q):
-        compare(cross + q * (2 - cross), first, 2 + q * (cross - 2), first, 2 + q)
+    compare(cross, first, 2, first, 2, back=2)
 
     relay(6)
     for part in (6, 7):
         spreads[part][0].wait_recv()
 
-    @pl.loop(0, 6)
+    @pl.loop(0, 2)
+    def _(q):
+        compare(0, first, q, last, q, own=True)
+
+    @pl.loop(0, 2)
     def _(i):
-        j = i // 2
-        q = lax.rem(i, 2)
-        compare(j + (j + 1) // 2, first, q, last, q, own=True)
+        compare(2 + i, first, beside_block(i), last, beside_block(i), back=i)
 
     @pl.loop(0, 2)
     def _(q):
@@ -310,23 +323,24 @@
     for part in (6, 7):
         spreads[part][1].wait_recv()
 
-    @pl.loop(0, 4)
+    @pl.loop(0, 2)
     def _(i):
-        q = lax.rem(i, 2)
-        compare(2 + i // 2, last, q, whole, q)
+        compare(2 + i, last, beside_block(i), whole, beside_block(i), back=i)
 
     relayed([relays[6], relays[7]], lambda copy: copy.wait_recv())
 
-    @pl.loop(0, 2)
-    def _(q):
-        compare(cross + q * (2 - cross), first, 2 + q * (cross - 2), last, 2 + q)
-
-    @pl.loop(0, 2)
-    def _(q):
-        compare(cross + q * (2 - cross), last, 2 + q * (cross - 2), whole, 2 + q)
+    compare(cross, first, 2, last, 2, back=2)
+    compare(cross, last, 2, whole, 2, back=2)
+
+    def turned(back):
+        return jnp.max(key_best[back].T, axis=0, keepdims=True)
+
+    best[2] = jnp.maximum(best[2], turned(0))
+    best[3] = turned(2)
+    best[4] = turned(1)
 
     copies = []
-    for h, device in enumerate((tile, sib, xdev, crossdev)):
+    for h, device in enumerate((tile, sib, xdev, crossdev, ydev)):
         for r in (3, 2, 1, 0):
             index = h * 4 + r
             if index == 0:
@@ -344,7 +358,8 @@
     for r in range(4):
         block = jnp.maximum(
             jnp.maximum(result_in[r], result_in[4 + r]), jnp.maximum(result_in[8 + r], result_in[12 + r])
-        )[:, r * cap : (r + 1) * cap]
+        )
+        block = jnp.maximum(block, result_in[16 + r])[:, r * cap : (r + 1) * cap]
         high = block.astype(jnp.bfloat16).astype(jnp.float32)
         middle = (block - high).astype(jnp.bfloat16).astype(jnp.float32)
         picks[r : r + 1, :] = high
@@ -385,14 +400,15 @@
             pltpu.VMEM((3, 8, slots), jnp.float32),
             pltpu.VMEM((5, 1, slots), jnp.float32),
             pltpu.VMEM((5, slots, 128), jnp.float32),
-            pltpu.VMEM((4, 1, slots), jnp.float32),
-            pltpu.VMEM((16, 1, slots), jnp.float32),
+            pltpu.VMEM((5, 1, slots), jnp.float32),
+            pltpu.VMEM((3, slots, 128), jnp.float32),
+            pltpu.VMEM((20, 1, slots), jnp.float32),
             pltpu.VMEM((16, slots // 4), jnp.float32),
             dma((3,)),
             dma((3,)), dma((3,)), dma((8,)), dma((8,)),
             dma((4,)), dma((4,)), dma((8,)), dma((8,)),
             dma((2, 8)), dma((2, 8)), dma((8,)), dma((8,)),
-            dma((16,)), dma((16,)),
+            dma((20,)), dma((20,)),
         ],
         compiler_params=pltpu.CompilerParams(
             collective_id=0, has_side_effects=True, vmem_limit_bytes=64 * 1024 * 1024 - 256 * 1024

time: 65.5 us -> 59.9 us (0.915)
  Pallas kernels: 64.1 us -> 58.4 us
    pallas_call x1, Pallas kernels: 64.1 us -> 58.4 us  [local_fused(): pl.pallas_call(kernel, out_shape=jax.ShapeDtypeStruct((rows,), jnp.float3...]
where the time goes in v8:
time: 59.9 us; the launch traced here: 59.7 us
  Pallas kernels  58.4 us (97%)
  local copies, waits for them, and re-layouts  1.26 us (2%)
    pallas_call x1, Pallas kernels, local_fused(): pl.pallas_call(kernel, out_shape=jax.ShapeDtypeStruct((rows,), jnp.float3...  58.4 us
    unnamed x1, local copies, waits for them, and re-layouts  1.26 us

profile of v8, /device:TPU:0, one launch (start us, length us, event | category | flops | bytes accessed | tf_op | source)
XLA Modules:
  0.0 59.7 jit_solution(857728750902974028)
XLA Ops:
  0.0 58.4 %shard_map.37 = f32[384]{0:T(512)} custom-call(bf16[384,1024]{1,0:T(8,128)(2,1)} %x_ref.1, s32[384]{0:T(512)} %owner_ref.1, s32[384]{0:T(512)} %cluster_ref.1), custom_call_target="tpu_custom_call" | custom-call | tf_op jit(solution)/shard_map/pallas_call | solution.py:387
  58.5 1.3 %copy.5 = f32[384]{0:T(512)} copy(f32[384]{0:T(512)} %shard_map.37) | data formatting | bytes 3072

commit v9 on v8

--- a/solution.py
+++ b/solution.py
@@ -141,7 +141,7 @@
         return jnp.dot(sel, normed[...], preferred_element_type=jnp.float32).astype(jnp.bfloat16)
 
     sixth = cap // 6
-    parts = ((0, 0, 6), (1, 0, 3), (1, 3, 6), (2, 0, 1), (2, 1, 3), (2, 3, 6), (3, 0, 3), (3, 3, 6))
+    parts = ((0, 0, 6), (1, 0, 3), (1, 3, 6), (2, 0, 1), (2, 1, 3), (2, 3, 6), (3, 0, 3), (3, 3, 5), (3, 5, 6))
 
     def begin(part):
         r, low, high = parts[part]
@@ -286,6 +286,8 @@
 
     for part in (0, 3, 1, 4, 2):
         relay(part)
+    zcopies[6].wait_send()
+    begin(8)
     spread(6)
     relay(5)
     for part in range(6):
@@ -299,12 +301,13 @@
         compare(2 + i, first, beside_block(i), first, beside_block(i), back=i)
 
     spread(7)
+    spread(8)
     relayed([relays[part] for part in range(6)], lambda copy: copy.wait_recv())
 
     compare(cross, first, 2, first, 2, back=2)
 
     relay(6)
-    for part in (6, 7):
+    for part in (6, 7, 8):
         spreads[part][0].wait_recv()
 
     @pl.loop(0, 2)
@@ -320,16 +323,16 @@
         compare(0, last, q, whole, q, own=True)
 
     relay(7)
-    for part in (6, 7):
+    relay(8)
+    for part in (6, 7, 8):
         spreads[part][1].wait_recv()
 
     @pl.loop(0, 2)
     def _(i):
         compare(2 + i, last, beside_block(i), whole, beside_block(i), back=i)
 
-    relayed([relays[6], relays[7]], lambda copy: copy.wait_recv())
-
     compare(cross, first, 2, last, 2, back=2)
+    relayed([relays[part] for part in (6, 7, 8)], lambda copy: copy.wait_recv())
     compare(cross, last, 2, whole, 2, back=2)
 
     def turned(back):
@@ -372,7 +375,7 @@
         out = jnp.where(owner == peer[r], value, out)
     out_ref[...] = out.reshape(rows)
 
-    for copy in ztags + ptags + copies + [zcopies[2], zcopies[6], zcopies[7]]:
+    for copy in ztags + ptags + copies + [zcopies[2], zcopies[7], zcopies[8]]:
         copy.wait_send()
     for group in spreads.values():
         for copy in group:
@@ -405,9 +408,9 @@
             pltpu.VMEM((20, 1, slots), jnp.float32),
             pltpu.VMEM((16, slots // 4), jnp.float32),
             dma((3,)),
-            dma((3,)), dma((3,)), dma((8,)), dma((8,)),
-            dma((4,)), dma((4,)), dma((8,)), dma((8,)),
-            dma((2, 8)), dma((2, 8)), dma((8,)), dma((8,)),
+            dma((3,)), dma((3,)), dma((9,)), dma((9,)),
+            dma((4,)), dma((4,)), dma((9,)), dma((9,)),
+            dma((2, 9)), dma((2, 9)), dma((9,)), dma((9,)),
             dma((20,)), dma((20,)),
         ],
         compiler_params=pltpu.CompilerParams(

time: 59.9 us -> 60.3 us (level)
  no operation moved by 1% of the time
where the time goes in v9:
time: 60.3 us; the launch traced here: 60.1 us
  Pallas kernels  58.8 us (98%)
  local copies, waits for them, and re-layouts  1.26 us (2%)
    pallas_call x1, Pallas kernels, local_fused(): pl.pallas_call(kernel, out_shape=jax.ShapeDtypeStruct((rows,), jnp.float3...  58.8 us
    unnamed x1, local copies, waits for them, and re-layouts  1.26 us

profile of v9, /device:TPU:0, one launch (start us, length us, event | category | flops | bytes accessed | tf_op | source)
XLA Modules:
  0.0 60.1 jit_solution(12779373690427691109)
XLA Ops:
  0.0 58.8 %shard_map.37 = f32[384]{0:T(512)} custom-call(bf16[384,1024]{1,0:T(8,128)(2,1)} %x_ref.1, s32[384]{0:T(512)} %owner_ref.1, s32[384]{0:T(512)} %cluster_ref.1), custom_call_target="tpu_custom_call" | custom-call | tf_op jit(solution)/shard_map/pallas_call | solution.py:390
  58.8 1.3 %copy.5 = f32[384]{0:T(512)} copy(f32[384]{0:T(512)} %shard_map.37) | data formatting | bytes 3072

commit v10 on v8

--- a/solution.py
+++ b/solution.py
@@ -327,20 +327,12 @@
     def _(i):
         compare(2 + i, last, beside_block(i), whole, beside_block(i), back=i)
 
-    relayed([relays[6], relays[7]], lambda copy: copy.wait_recv())
-
-    compare(cross, first, 2, last, 2, back=2)
-    compare(cross, last, 2, whole, 2, back=2)
-
     def turned(back):
         return jnp.max(key_best[back].T, axis=0, keepdims=True)
 
-    best[2] = jnp.maximum(best[2], turned(0))
-    best[3] = turned(2)
-    best[4] = turned(1)
-
     copies = []
-    for h, device in enumerate((tile, sib, xdev, crossdev, ydev)):
+
+    def give(h, device):
         for r in (3, 2, 1, 0):
             index = h * 4 + r
             if index == 0:
@@ -351,6 +343,20 @@
             )
             copy.start()
             copies.append(copy)
+
+    give(0, tile)
+    give(1, sib)
+    best[4] = turned(1)
+    give(4, ydev)
+
+    compare(cross, first, 2, last, 2, back=2)
+    relayed([relays[6], relays[7]], lambda copy: copy.wait_recv())
+    compare(cross, last, 2, whole, 2, back=2)
+
+    best[3] = turned(2)
+    give(3, crossdev)
+    best[2] = jnp.maximum(best[2], turned(0))
+    give(2, xdev)
     for copy in copies:
         copy.wait_recv()
 

time: 59.9 us -> 60.2 us (level)
  no operation moved by 1% of the time
where the time goes in v10:
time: 60.2 us; the launch traced here: 60 us
  Pallas kernels  58.8 us (98%)
  local copies, waits for them, and re-layouts  1.26 us (2%)
    pallas_call x1, Pallas kernels, local_fused(): pl.pallas_call(kernel, out_shape=jax.ShapeDtypeStruct((rows,), jnp.float3...  58.8 us
    unnamed x1, local copies, waits for them, and re-layouts  1.26 us

profile of v10, /device:TPU:0, one launch (start us, length us, event | category | flops | bytes accessed | tf_op | source)
XLA Modules:
  0.0 60.0 jit_solution(7563796434032244756)
XLA Ops:
  0.0 58.8 %shard_map.37 = f32[384]{0:T(512)} custom-call(bf16[384,1024]{1,0:T(8,128)(2,1)} %x_ref.1, s32[384]{0:T(512)} %owner_ref.1, s32[384]{0:T(512)} %cluster_ref.1), custom_call_target="tpu_custom_call" | custom-call | tf_op jit(solution)/shard_map/pallas_call | solution.py:393
  58.8 1.3 %copy.5 = f32[384]{0:T(512)} copy(f32[384]{0:T(512)} %shard_map.37) | data formatting | bytes 3072
